TPU v7x, 128 devices: a whole 4x4x4 slice. The times are simulated.
128 devices in a mesh: group: 8 (over x_lo, y), dev: 16 (over x_hi, z, core).
Axes of the slice: x: 4 (x_hi: 2, x_lo: 2; x = x_hi * 2 + x_lo), y: 4, z: 4, core: 2. Of those that a mesh axis runs over, the one named last changes fastest.
Arguments:
- x_act: bfloat16 [40960, 4608], P(('group', 'dev')), may hold values from -2 to 2
- cotangent: bfloat16 [40960, 1024], P(('group', 'dev')), may hold values from -0.5 to 0.5
- sign_bits: int32 [1024], replicated, may hold values from 0 to 1
Outputs:
- rotated_sum: bfloat16 [4608, 1024], P('dev', 'group')
- mean_grad: bfloat16 [4608, 1024], replicated
All inputs are finite; a program needn't handle non-finite values.
Results may differ from a plain program's by a relative error of at most 0.001.
Values may be sent and summed in bfloat16 or wider, within the bound.
A program may use at most 128 MiB of HBM per device.

v0:
```python
import jax
import jax.numpy as jnp
from jax import lax
from jax.sharding import PartitionSpec as P

BLOCK = 128


def passed_along(value, axis, steps):
    count = lax.axis_size(axis)
    leading, last = (max(0, -steps), min(count, count - steps))
    return lax.ppermute(value, axis, [(source, source + steps) for source in range(leading, last)])


def from_root(x, axis, root):
    mine = lax.axis_index(axis) == root
    return lax.psum(jnp.where(mine, x, jnp.zeros_like(x)), axis)


def hadamard():
    index_vals = jnp.arange(BLOCK)
    both = jnp.bitwise_and(index_vals[:, None], index_vals[None, :])
    parity = jnp.zeros_like(both)
    for bit_pos in range(7):
        parity = parity + jnp.bitwise_and(jnp.right_shift(both, bit_pos), 1)
    return (1 - 2 * (parity % 2)).astype(jnp.float32)


def rotate(matrix, signs, hmat):
    rows = matrix.shape[0]
    blocks = (matrix * signs[None, :]).reshape(rows, -1, BLOCK)
    turned = jnp.einsum("rbi,ij->rbj", blocks, hmat, precision=lax.Precision.HIGHEST)
    return turned.reshape(rows, -1)


def unrotate(matrix, signs, hmat):
    rows = matrix.shape[0]
    blocks = matrix.reshape(rows, -1, BLOCK)
    turned = jnp.einsum("rbi,ij->rbj", blocks, hmat, precision=lax.Precision.HIGHEST)
    return (turned / BLOCK).reshape(rows, -1) * signs[None, :]


def quantize(matrix):
    shape = matrix.shape
    blocks = matrix.reshape(shape[:-1] + (shape[-1] // BLOCK, BLOCK))
    largest = jnp.max(jnp.abs(blocks), axis=-1)
    powers = jnp.asarray([2.0**k for k in range(-7, 31)], dtype=jnp.float32)
    exceeds = largest[..., None] > 63.5 * powers
    scales = jnp.max(jnp.where(exceeds, powers, 0.00390625), axis=-1).astype(jnp.bfloat16)
    ratio = blocks / scales.astype(jnp.float32)[..., None]
    floored = jnp.floor(ratio)
    fraction = ratio - floored
    odd_level = floored - 2.0 * jnp.floor(0.5 * floored) == 1.0
    round_up = (fraction > 0.5) | (fraction == 0.5) & odd_level
    levels = (floored + round_up.astype(jnp.float32)).astype(jnp.bfloat16)
    return (levels.reshape(shape), scales)


def dequant(levels, scales):
    shape = levels.shape
    blocks = levels.astype(jnp.float32).reshape(shape[:-1] + (shape[-1] // BLOCK, BLOCK))
    return (blocks * scales.astype(jnp.float32)[..., None]).reshape(shape)


def body(x_act, cotangent, sign_bits):
    signs = (2 * sign_bits - 1).astype(jnp.float32)
    hmat = hadamard()
    local = lax.dot_general(
        x_act, cotangent, (((0,), (0,)), ((), ())), preferred_element_type=jnp.float32
    )
    levels, scales = quantize(rotate(local, signs, hmat))
    width = levels.shape[1]
    members = lax.axis_size("dev")
    groups = lax.axis_size("group")
    rows = levels.shape[0] // members
    got_levels, got_scales = (
        lax.all_to_all(
            levels.reshape(members, rows, width), "dev", split_axis=0, concat_axis=0, tiled=True
        ),
        lax.all_to_all(
            scales.reshape(members, rows, width // BLOCK),
            "dev",
            split_axis=0,
            concat_axis=0,
            tiled=True,
        ),
    )
    group_total = jnp.sum(dequant(got_levels, got_scales), axis=0)
    own = quantize(group_total)
    position = lax.axis_index("group")

    def one_hop(step_idx, carry):
        arrived = passed_along((carry[0], carry[1]), "group", 1)
        merged = quantize(dequant(*arrived) + dequant(*own))
        chosen = position == step_idx
        return (jnp.where(chosen, merged[0], carry[0]), jnp.where(chosen, merged[1], carry[1]))

    running = lax.fori_loop(1, groups, one_hop, own)
    final = (from_root(running[0], "group", groups - 1), from_root(running[1], "group", groups - 1))
    total = dequant(*final) / (groups * members)
    column_share = width // groups
    own_columns = lax.dynamic_slice_in_dim(total, position * column_share, column_share, 1)
    rotated_sum = own_columns.astype(jnp.bfloat16)
    all_levels, all_scales = (
        lax.all_gather(final[0], "dev", axis=0, tiled=True),
        lax.all_gather(final[1], "dev", axis=0, tiled=True),
    )
    everything = dequant(all_levels, all_scales) / (groups * members)
    mean_grad = unrotate(everything, signs, hmat).astype(jnp.bfloat16)
    return (rotated_sum, mean_grad)


def solution(mesh):
    placed = (P(("group", "dev"), None), P(("group", "dev"), None), P())
    return jax.shard_map(
        body, mesh=mesh, in_specs=placed, out_specs=(P("dev", "group"), P()), check_vma=False
    )
```

profile of v0, /device:TPU:1, one launch (start us, length us, event | category | flops | bytes accessed | tf_op | source)
XLA Modules:
  0.0 666.9 jit_solution(3309656394618254053)
XLA Ops:
  9.0 6.3 broadcast_multiply_fusion
  15.4 23.5 %abs_reduce_fusion = (f32[4608,8]{0,1:T(8,128)S(1)}, f32[4608,8,128]{0,2,1:T(8,128)}) fusion(f32[4608,8,128]{0,2,1:T(8,128)S(1)} %bitcast.102), kind=kOutput, calls=%fused_computation.34 | convolution fusion | flops 7257731072 | bytes 37896192 | tf_op jit(solution)/shard_map/rbi,ij->rbj/dot_general | solution.py:32
  40.4 9.3 %all-to-all-start.1 = ((bf16[16,288,8]{1,2,0:T(8,128)(2,1)}), bf16[16,288,8]{1,2,0:T(8,128)(2,1)S(1)}, u32[]{:S(2)}, u32[]{:S(2)}) async-start(bf16[16,288,8]{1,2,0:T(8,128)(2,1)} %copy.53), calls=%async_computation.1 | async-start | bytes 196608 | tf_op jit(solution)/shard_map/all_to_all | solution.py:80
  49.7 14.2 %fusion.8 = bf16[4608,8,128]{0,2,1:T(8,128)(2,1)} fusion(f32[4608,8,128]{0,2,1:T(8,128)} %get-tuple-element.187, f32[4608,8]{0,1:T(8,128)S(1)} %convert_element_type.155), kind=kLoop, calls=%fused_computation.24 | loop fusion | flops 70778880 | bytes 28459008 | tf_op jit(solution)/shard_map/convert_element_type | solution.py:55
  63.9 12.9 %copy.52 = bf16[4608,8,128]{2,1,0:T(8,128)(2,1)} copy(bf16[4608,8,128]{0,2,1:T(8,128)(2,1)} %fusion.8) | data formatting | bytes 18874368 | tf_op jit(solution)/shard_map/convert_element_type | solution.py:55
  76.8 14.8 %reshape_reshape.3 = bf16[16,288,1024]{2,1,0:T(8,128)(2,1)} reshape(bf16[4608,8,128]{2,1,0:T(8,128)(2,1)} %copy.52) | data formatting | bytes 18874368 | tf_op jit(solution)/shard_map/reshape;reshape | solution.py:78
  91.5 7.2 %all-to-all-start = ((bf16[16,288,1024]{2,1,0:T(8,128)(2,1)}), bf16[16,288,1024]{2,1,0:T(8,128)(2,1)}, u32[]{:S(2)}, u32[]{:S(2)}) async-start(bf16[16,288,1024]{2,1,0:T(8,128)(2,1)} %reshape_reshape.3), calls=%async_computation | async-start | bytes 18874368 | tf_op jit(solution)/shard_map/all_to_all | solution.py:77
  99.2 7.4 %mul.164 = f32[16,288,8,128]{3,2,1,0:T(8,128)} broadcast(f32[16,288,8]{2,1,0:T(8,128)S(1)} %copy.54), dimensions={0,1,2} | broadcast | bytes 19021824 | tf_op jit(solution)/shard_map/mul | solution.py:62
  106.6 20.2 %mul.165 = f32[16,288,1024]{2,1,0:T(8,128)} reshape(f32[16,288,8,128]{3,2,1,0:T(8,128)} %mul.164) | data formatting | bytes 37748736 | tf_op jit(solution)/shard_map/mul | solution.py:62
  126.9 108.2 %all-to-all-done = bf16[16,288,1024]{2,1,0:T(8,128)(2,1)} async-done(((bf16[16,288,1024]{2,1,0:T(8,128)(2,1)}), bf16[16,288,1024]{2,1,0:T(8,128)(2,1)}, u32[]{:S(2)}, u32[]{:S(2)}) %all-to-all-start) | async-done | bytes 9437216 | tf_op jit(solution)/shard_map/all_to_all | solution.py:77
  235.1 10.2 %multiply_reduce_fusion = f32[288,1024]{1,0:T(8,128)S(1)} fusion(f32[16,288,1024]{2,1,0:T(8,128)} %mul.165, bf16[16,288,1024]{2,1,0:T(8,128)(2,1)} %all-to-all-done), kind=kLoop, calls=%fused_computation.33 | loop fusion | flops 13860864 | bytes 29491200 | tf_op jit(solution)/shard_map/reduce_sum | solution.py:88
  249.0 165.1 %while.16 = (s32[]{:T(128)}, bf16[288,1024]{1,0:T(8,128)(2,1)}, bf16[288,8]{0,1:T(8,128)(2,1)S(1)}, s32[]{:T(128)}, bf16[288,1024]{1,0:T(8,128)(2,1)S(1)}, /*ind...) while((s32[]{:T(128)}, bf16[288,1024]{1,0:T(8,128)(2,1)}, ...), condition=%wide.region_8.9_spmd.clone, body=%wide.region_5.8_spmd.sunk.clone.sunk | while | flops 8517891 | bytes 27256824 | solution.py:98
  249.0 3.2 collective-permute-start.1
  252.2 3.2 collective-permute-start
  255.4 9.0 %collective-permute-done = bf16[288,8]{0,1:T(8,128)(2,1)S(1)} collective-permute-done((bf16[288,8]{0,1:T(8,128)(2,1)S(1)}, bf16[288,8]{0,1:T(8,128)(2,1)S(1)}, u32[]{:S(2)}, u32[]{:S(2)}) %collective-permute-start) | collective-permute-done | bytes 4640 | tf_op jit(solution)/shard_map/while/body/eval_jaxpr/ppermute | solution.py:12
  270.5 3.5 broadcast_select_fusion.6
  273.9 4.0 collective-permute-start.1
  277.9 3.3 collective-permute-start
  281.2 7.9 %collective-permute-done = bf16[288,8]{0,1:T(8,128)(2,1)S(1)} collective-permute-done((bf16[288,8]{0,1:T(8,128)(2,1)S(1)}, bf16[288,8]{0,1:T(8,128)(2,1)S(1)}, u32[]{:S(2)}, u32[]{:S(2)}) %collective-permute-start) | collective-permute-done | bytes 4640 | tf_op jit(solution)/shard_map/while/body/eval_jaxpr/ppermute | solution.py:12
  295.2 3.5 broadcast_select_fusion.6
  298.7 4.1 collective-permute-start.1
  302.8 3.2 collective-permute-start
  306.0 7.1 %collective-permute-done = bf16[288,8]{0,1:T(8,128)(2,1)S(1)} collective-permute-done((bf16[288,8]{0,1:T(8,128)(2,1)S(1)}, bf16[288,8]{0,1:T(8,128)(2,1)S(1)}, u32[]{:S(2)}, u32[]{:S(2)}) %collective-permute-start) | collective-permute-done | bytes 4640 | tf_op jit(solution)/shard_map/while/body/eval_jaxpr/ppermute | solution.py:12
  319.3 3.5 broadcast_select_fusion.6
  322.7 4.1 collective-permute-start.1
  326.9 3.2 collective-permute-start
  330.0 6.2 collective-permute-done
  342.4 3.5 broadcast_select_fusion.6
  345.8 4.1 collective-permute-start.1
  350.0 5.2 collective-permute-start
  355.2 3.2 collective-permute-done
  364.6 3.5 broadcast_select_fusion.6
  368.0 5.5 collective-permute-start.1
  373.6 6.4 collective-permute-start
  387.4 3.5 broadcast_select_fusion.6
  390.9 6.5 collective-permute-start.1
  397.4 6.1 collective-permute-start
  410.6 3.5 broadcast_select_fusion.6
  415.0 99.9 %all-reduce.2.cloned.1.call-done = bf16[288,1024]{1,0:T(8,128)(2,1)} async-done(((bf16[288,1024]{1,0:T(8,128)(2,1)}), bf16[288,1024]{1,0:T(8,128)(2,1)}) %all-reduce.2.cloned.1.call-update) | async-done | bytes 589840 | tf_op jit(solution)/shard_map/psum | solution.py:17
  515.0 14.1 %psum.15 = bf16[288,8]{0,1:T(8,128)(2,1)S(1)} all-reduce(bf16[288,8]{0,1:T(8,128)(2,1)S(1)} %broadcast_select_fusion.3), channel_id=1, replica_groups=mesh['group'=8,'dev'=16] {'group'}, use_global_device_ids=true, to_apply=%region_10.11 | all-reduce | flops 2304 | bytes 9216 | tf_op jit(solution)/shard_map/psum | solution.py:17
  529.8 35.1 %all-gather = bf16[16,288,8]{1,2,0:T(8,128)(2,1)} all-gather(bf16[1,288,8]{1,2,0:T(8,128)(2,1)S(1)} %bitcast.111), channel_id=1, replica_groups=mesh['group'=8,'dev'=16] {'dev'}, dimensions={0}, use_global_device_ids=true | all-gather | bytes 78336 | tf_op jit(solution)/shard_map/all_gather | solution.py:106
  565.0 1.3 copy.64
  566.3 1.6 fusion.23
  567.8 32.4 %all-gather.3.cloned.1.call-done = bf16[4608,1024]{1,0:T(8,128)(2,1)} async-done(((bf16[288,1024]{1,0:T(8,128)(2,1)}), bf16[4608,1024]{1,0:T(8,128)(2,1)}) %all-gather.3.cloned.1.call-update) | async-done | bytes 9437200 | tf_op jit(solution)/shard_map/all_gather | solution.py:105
  600.2 7.0 %mul.174 = f32[4608,8,128]{2,1,0:T(8,128)} broadcast(f32[4608,8]{1,0:T(8,128)S(1)} %bitcast.106), dimensions={0,1} | broadcast | bytes 19021824 | tf_op jit(solution)/shard_map/mul | solution.py:62
  607.2 28.6 %fusion.15 = f32[4608,8,128]{0,2,1:T(8,128)} fusion(f32[576,8,8,128]{3,2,1,0:T(8,128)} %bitcast.105, bf16[4608,1024]{1,0:T(8,128)(2,1)} %all-gather.3.cloned.1.call-done), kind=kOutput, calls=%fused_computation.35 | convolution fusion | flops 7267205120 | bytes 47185920 | tf_op jit(solution)/shard_map/rbi,ij->rbj/dot_general | solution.py:39
  635.8 11.6 %fusion.14 = bf16[4608,1024]{0,1:T(8,128)(2,1)} fusion(f32[4608,8,128]{0,2,1:T(8,128)} %fusion.15, f32[1024]{0:T(1024)S(1)} %add_convert_fusion), kind=kLoop, calls=%fused_computation.32 | loop fusion | flops 9437184 | bytes 28315648 | tf_op jit(solution)/shard_map/convert_element_type | solution.py:109
  647.3 12.7 %copy.62 = bf16[4608,1024]{1,0:T(8,128)(2,1)} copy(bf16[4608,1024]{0,1:T(8,128)(2,1)} %fusion.14) | data formatting | bytes 18874368
  (162 shorter events, 53.7 us)
Async XLA Ops:
  7.2 1.9 copy-start
  15.4 23.6 %copy-start.5 = (bf16[38]{0:T(256)(128)(2,1)S(1)}, bf16[38]{0:T(256)(128)(2,1)}, u32[]{:S(2)}) copy-start(bf16[38]{0:T(256)(128)(2,1)} %constant.195) | copy-start | bytes 232
  15.4 23.5 %copy-start.6 = (f32[38]{0:T(128)S(1)}, f32[38]{0:T(128)}, u32[]{:S(2)}) copy-start(f32[38]{0:T(128)} %constant.122) | copy-start | bytes 460
  40.4 51.1 %all-to-all-start.1 = ((bf16[16,288,8]{1,2,0:T(8,128)(2,1)}), bf16[16,288,8]{1,2,0:T(8,128)(2,1)S(1)}, u32[]{:S(2)}, u32[]{:S(2)}) async-start(bf16[16,288,8]{1,2,0:T(8,128)(2,1)} %copy.53), calls=%async_computation.1 | async-start | bytes 196608 | tf_op jit(solution)/shard_map/all_to_all | solution.py:80
  91.5 143.5 %all-to-all-start = ((bf16[16,288,1024]{2,1,0:T(8,128)(2,1)}), bf16[16,288,1024]{2,1,0:T(8,128)(2,1)}, u32[]{:S(2)}, u32[]{:S(2)}) async-start(bf16[16,288,1024]{2,1,0:T(8,128)(2,1)} %reshape_reshape.3), calls=%async_computation | async-start | bytes 18874368 | tf_op jit(solution)/shard_map/all_to_all | solution.py:77
  98.8 416.2 %all-reduce.2.cloned.1.call-start = ((), (), s32[]{:S(2)}) async-start(), calls=%async_computation.2 | async-start | bytes 1179648 | tf_op jit(solution)/shard_map/psum | solution.py:17
  249.0 17.1 %copy-start.2 = (bf16[288,1024]{1,0:T(8,128)(2,1)}, bf16[288,1024]{1,0:T(8,128)(2,1)S(1)}, u32[]{:S(2)}) copy-start(bf16[288,1024]{1,0:T(8,128)(2,1)S(1)} %get-tuple-element.249) | copy-start | bytes 1769476 | tf_op jit(solution)/shard_map/while
  249.0 15.5 %collective-permute-start.1 = (bf16[288,1024]{1,0:T(8,128)(2,1)}, bf16[288,1024]{1,0:T(8,128)(2,1)S(1)}, u32[]{:S(2)}, u32[]{:S(2)}) collective-permute-start(bf16[288,1024]{1,0:T(8,128)(2,1)} %get-tuple-element.236), channel_id=1, source_target_pairs={{0,16},{16,32},{32,48},{48,64},{64,80},{80,96},{96,112},{1,17},{17... | collective-permute-start | bytes 1769480 | tf_op jit(solution)/shard_map/while/body/eval_jaxpr/ppermute | solution.py:12
  252.2 12.1 %collective-permute-start = (bf16[288,8]{0,1:T(8,128)(2,1)S(1)}, bf16[288,8]{0,1:T(8,128)(2,1)S(1)}, u32[]{:S(2)}, u32[]{:S(2)}) collective-permute-start(bf16[288,8]{0,1:T(8,128)(2,1)S(1)} %get-tuple-element.237), channel_id=1, source_target_pairs={{0,16},{16,32},{32,48},{48,64},{64,80},{80,96},{96,112},{1,17},{17... | collective-permute-start | bytes 13832 | tf_op jit(solution)/shard_map/while/body/eval_jaxpr/ppermute | solution.py:12
  264.5 1.6 copy-start.4
  270.5 3.5 copy-start.3
  273.9 16.9 %copy-start.2 = (bf16[288,1024]{1,0:T(8,128)(2,1)}, bf16[288,1024]{1,0:T(8,128)(2,1)S(1)}, u32[]{:S(2)}) copy-start(bf16[288,1024]{1,0:T(8,128)(2,1)S(1)} %get-tuple-element.249) | copy-start | bytes 1769476 | tf_op jit(solution)/shard_map/while
  273.9 15.3 %collective-permute-start.1 = (bf16[288,1024]{1,0:T(8,128)(2,1)}, bf16[288,1024]{1,0:T(8,128)(2,1)S(1)}, u32[]{:S(2)}, u32[]{:S(2)}) collective-permute-start(bf16[288,1024]{1,0:T(8,128)(2,1)} %get-tuple-element.236), channel_id=1, source_target_pairs={{0,16},{16,32},{32,48},{48,64},{64,80},{80,96},{96,112},{1,17},{17... | collective-permute-start | bytes 1769480 | tf_op jit(solution)/shard_map/while/body/eval_jaxpr/ppermute | solution.py:12
  277.9 11.2 %collective-permute-start = (bf16[288,8]{0,1:T(8,128)(2,1)S(1)}, bf16[288,8]{0,1:T(8,128)(2,1)S(1)}, u32[]{:S(2)}, u32[]{:S(2)}) collective-permute-start(bf16[288,8]{0,1:T(8,128)(2,1)S(1)} %get-tuple-element.237), channel_id=1, source_target_pairs={{0,16},{16,32},{32,48},{48,64},{64,80},{80,96},{96,112},{1,17},{17... | collective-permute-start | bytes 13832 | tf_op jit(solution)/shard_map/while/body/eval_jaxpr/ppermute | solution.py:12
  289.2 1.6 copy-start.4
  295.2 3.5 copy-start.3
  298.7 16.2 %copy-start.2 = (bf16[288,1024]{1,0:T(8,128)(2,1)}, bf16[288,1024]{1,0:T(8,128)(2,1)S(1)}, u32[]{:S(2)}) copy-start(bf16[288,1024]{1,0:T(8,128)(2,1)S(1)} %get-tuple-element.249) | copy-start | bytes 1769476 | tf_op jit(solution)/shard_map/while
  298.7 14.5 %collective-permute-start.1 = (bf16[288,1024]{1,0:T(8,128)(2,1)}, bf16[288,1024]{1,0:T(8,128)(2,1)S(1)}, u32[]{:S(2)}, u32[]{:S(2)}) collective-permute-start(bf16[288,1024]{1,0:T(8,128)(2,1)} %get-tuple-element.236), channel_id=1, source_target_pairs={{0,16},{16,32},{32,48},{48,64},{64,80},{80,96},{96,112},{1,17},{17... | collective-permute-start | bytes 1769480 | tf_op jit(solution)/shard_map/while/body/eval_jaxpr/ppermute | solution.py:12
  302.8 10.3 %collective-permute-start = (bf16[288,8]{0,1:T(8,128)(2,1)S(1)}, bf16[288,8]{0,1:T(8,128)(2,1)S(1)}, u32[]{:S(2)}, u32[]{:S(2)}) collective-permute-start(bf16[288,8]{0,1:T(8,128)(2,1)S(1)} %get-tuple-element.237), channel_id=1, source_target_pairs={{0,16},{16,32},{32,48},{48,64},{64,80},{80,96},{96,112},{1,17},{17... | collective-permute-start | bytes 13832 | tf_op jit(solution)/shard_map/while/body/eval_jaxpr/ppermute | solution.py:12
  313.3 1.6 copy-start.4
  319.3 3.5 copy-start.3
  322.7 15.3 %copy-start.2 = (bf16[288,1024]{1,0:T(8,128)(2,1)}, bf16[288,1024]{1,0:T(8,128)(2,1)S(1)}, u32[]{:S(2)}) copy-start(bf16[288,1024]{1,0:T(8,128)(2,1)S(1)} %get-tuple-element.249) | copy-start | bytes 1769476 | tf_op jit(solution)/shard_map/while
  322.7 13.6 %collective-permute-start.1 = (bf16[288,1024]{1,0:T(8,128)(2,1)}, bf16[288,1024]{1,0:T(8,128)(2,1)S(1)}, u32[]{:S(2)}, u32[]{:S(2)}) collective-permute-start(bf16[288,1024]{1,0:T(8,128)(2,1)} %get-tuple-element.236), channel_id=1, source_target_pairs={{0,16},{16,32},{32,48},{48,64},{64,80},{80,96},{96,112},{1,17},{17... | collective-permute-start | bytes 1769480 | tf_op jit(solution)/shard_map/while/body/eval_jaxpr/ppermute | solution.py:12
  326.9 9.4 %collective-permute-start = (bf16[288,8]{0,1:T(8,128)(2,1)S(1)}, bf16[288,8]{0,1:T(8,128)(2,1)S(1)}, u32[]{:S(2)}, u32[]{:S(2)}) collective-permute-start(bf16[288,8]{0,1:T(8,128)(2,1)S(1)} %get-tuple-element.237), channel_id=1, source_target_pairs={{0,16},{16,32},{32,48},{48,64},{64,80},{80,96},{96,112},{1,17},{17... | collective-permute-start | bytes 13832 | tf_op jit(solution)/shard_map/while/body/eval_jaxpr/ppermute | solution.py:12
  336.4 1.6 copy-start.4
  342.4 3.5 copy-start.3
  345.8 14.3 %copy-start.2 = (bf16[288,1024]{1,0:T(8,128)(2,1)}, bf16[288,1024]{1,0:T(8,128)(2,1)S(1)}, u32[]{:S(2)}) copy-start(bf16[288,1024]{1,0:T(8,128)(2,1)S(1)} %get-tuple-element.249) | copy-start | bytes 1769476 | tf_op jit(solution)/shard_map/while
  345.8 12.7 %collective-permute-start.1 = (bf16[288,1024]{1,0:T(8,128)(2,1)}, bf16[288,1024]{1,0:T(8,128)(2,1)S(1)}, u32[]{:S(2)}, u32[]{:S(2)}) collective-permute-start(bf16[288,1024]{1,0:T(8,128)(2,1)} %get-tuple-element.236), channel_id=1, source_target_pairs={{0,16},{16,32},{32,48},{48,64},{64,80},{80,96},{96,112},{1,17},{17... | collective-permute-start | bytes 1769480 | tf_op jit(solution)/shard_map/while/body/eval_jaxpr/ppermute | solution.py:12
  350.0 8.5 %collective-permute-start = (bf16[288,8]{0,1:T(8,128)(2,1)S(1)}, bf16[288,8]{0,1:T(8,128)(2,1)S(1)}, u32[]{:S(2)}, u32[]{:S(2)}) collective-permute-start(bf16[288,8]{0,1:T(8,128)(2,1)S(1)} %get-tuple-element.237), channel_id=1, source_target_pairs={{0,16},{16,32},{32,48},{48,64},{64,80},{80,96},{96,112},{1,17},{17... | collective-permute-start | bytes 13832 | tf_op jit(solution)/shard_map/while/body/eval_jaxpr/ppermute | solution.py:12
  358.6 1.6 copy-start.4
  364.6 3.5 copy-start.3
  368.0 15.0 %copy-start.2 = (bf16[288,1024]{1,0:T(8,128)(2,1)}, bf16[288,1024]{1,0:T(8,128)(2,1)S(1)}, u32[]{:S(2)}) copy-start(bf16[288,1024]{1,0:T(8,128)(2,1)S(1)} %get-tuple-element.249) | copy-start | bytes 1769476 | tf_op jit(solution)/shard_map/while
  368.0 13.4 %collective-permute-start.1 = (bf16[288,1024]{1,0:T(8,128)(2,1)}, bf16[288,1024]{1,0:T(8,128)(2,1)S(1)}, u32[]{:S(2)}, u32[]{:S(2)}) collective-permute-start(bf16[288,1024]{1,0:T(8,128)(2,1)} %get-tuple-element.236), channel_id=1, source_target_pairs={{0,16},{16,32},{32,48},{48,64},{64,80},{80,96},{96,112},{1,17},{17... | collective-permute-start | bytes 1769480 | tf_op jit(solution)/shard_map/while/body/eval_jaxpr/ppermute | solution.py:12
  373.6 7.7 %collective-permute-start = (bf16[288,8]{0,1:T(8,128)(2,1)S(1)}, bf16[288,8]{0,1:T(8,128)(2,1)S(1)}, u32[]{:S(2)}, u32[]{:S(2)}) collective-permute-start(bf16[288,8]{0,1:T(8,128)(2,1)S(1)} %get-tuple-element.237), channel_id=1, source_target_pairs={{0,16},{16,32},{32,48},{48,64},{64,80},{80,96},{96,112},{1,17},{17... | collective-permute-start | bytes 13832 | tf_op jit(solution)/shard_map/while/body/eval_jaxpr/ppermute | solution.py:12
  381.4 1.6 copy-start.4
  387.4 3.5 copy-start.3
  390.9 15.4 %copy-start.2 = (bf16[288,1024]{1,0:T(8,128)(2,1)}, bf16[288,1024]{1,0:T(8,128)(2,1)S(1)}, u32[]{:S(2)}) copy-start(bf16[288,1024]{1,0:T(8,128)(2,1)S(1)} %get-tuple-element.249) | copy-start | bytes 1769476 | tf_op jit(solution)/shard_map/while
  390.9 13.7 %collective-permute-start.1 = (bf16[288,1024]{1,0:T(8,128)(2,1)}, bf16[288,1024]{1,0:T(8,128)(2,1)S(1)}, u32[]{:S(2)}, u32[]{:S(2)}) collective-permute-start(bf16[288,1024]{1,0:T(8,128)(2,1)} %get-tuple-element.236), channel_id=1, source_target_pairs={{0,16},{16,32},{32,48},{48,64},{64,80},{80,96},{96,112},{1,17},{17... | collective-permute-start | bytes 1769480 | tf_op jit(solution)/shard_map/while/body/eval_jaxpr/ppermute | solution.py:12
  397.4 7.1 %collective-permute-start = (bf16[288,8]{0,1:T(8,128)(2,1)S(1)}, bf16[288,8]{0,1:T(8,128)(2,1)S(1)}, u32[]{:S(2)}, u32[]{:S(2)}) collective-permute-start(bf16[288,8]{0,1:T(8,128)(2,1)S(1)} %get-tuple-element.237), channel_id=1, source_target_pairs={{0,16},{16,32},{32,48},{48,64},{64,80},{80,96},{96,112},{1,17},{17... | collective-permute-start | bytes 13832 | tf_op jit(solution)/shard_map/while/body/eval_jaxpr/ppermute | solution.py:12
  404.6 1.6 copy-start.4
  410.6 3.5 copy-start.3
  415.0 185.2 %all-gather.3.cloned.1.call-start = ((), (), s32[]{:S(2)}) async-start(), calls=%async_computation.3 | async-start | bytes 10027008 | tf_op jit(solution)/shard_map/all_gather | solution.py:105
  647.3 12.8 %copy-start.1 = (bf16[320,4608]{1,0:T(8,128)(2,1)S(1)}, bf16[320,4608]{1,0:T(8,128)(2,1)}, u32[]{:S(2)}) copy-start(bf16[320,4608]{1,0:T(8,128)(2,1)} %param.8) | copy-start | bytes 8847364
Sparse Core Ops, SparseCore 0:
  415.1 99.8 all-reduce.1
  517.5 82.7 all-gather.2
where the time goes:
time: 670 us; the launch traced here: 667 us
  waiting for transfers between devices  276 us (41%)
  local copies, waits for them, and re-layouts  105 us (16%)
  other arithmetic  83.8 us (13%)
  starting transfers between devices  78.8 us (12%)
  matrix products  58.4 us (9%)
  blocking collectives  49.2 us (7%)
  between operations  14.2 us (2%)
    all_to_all x1, waiting for transfers between devices, body(): lax.all_to_all(levels.reshape(members, rows, width), 'dev', split_axis=0,...  108 us
    psum x1, waiting for transfers between devices, from_root(): return lax.psum(jnp.where(mine, x, jnp.zeros_like(x)), axis)  99.9 us
    ppermute x14, starting transfers between devices, passed_along(): lax.ppermute(value, axis, [(source, source + steps) for source in range(l...  62.2 us
    mul x18, local copies, waits for them, and re-layouts, dequant(): return (blocks * scales.astype(jnp.float32)[..., None]).reshape(shape)  46.3 us
    ppermute x14, waiting for transfers between devices, passed_along(): lax.ppermute(value, axis, [(source, source + steps) for source in range(l...  35.7 us
    all_gather x1, blocking collectives, body(): lax.all_gather(final[1], 'dev', axis=0, tiled=True)  35.1 us
    all_gather x1, waiting for transfers between devices, body(): lax.all_gather(final[0], 'dev', axis=0, tiled=True)  32.4 us
    dot_general x1, matrix products, unrotate(): jnp.einsum('rbi,ij->rbj', blocks, hmat, precision=lax.Precision.HIGHEST)  28.6 us
  transfers between devices with their start and end apart: 18, of which 10 were waited for; matrix products, arithmetic and copies ran while one was open for 11% of the time, Pallas kernels for 0%

commit v1 on v0

--- a/solution.py
+++ b/solution.py
@@ -1,9 +1,564 @@
+import functools
+
 import jax
 import jax.numpy as jnp
 from jax import lax
+from jax.experimental import pallas as pl
+from jax.experimental.pallas import tpu as pltpu
 from jax.sharding import PartitionSpec as P
 
 BLOCK = 128
+TOK = 320
+D = 4608
+KVW = 1024
+STAGES = 9
+QUAD = 1152
+OWN = 288
+PART = 96
+MAGIC = 12582912.0
+MESH = pl.DeviceIdType.MESH
+
+
+def hadamard_in_kernel():
+    i = lax.broadcasted_iota(jnp.int32, (BLOCK, BLOCK), 0)
+    j = lax.broadcasted_iota(jnp.int32, (BLOCK, BLOCK), 1)
+    both = i & j
+    parity = jnp.zeros_like(both)
+    for bit in range(7):
+        parity = parity + ((both >> bit) & 1)
+    return (1 - 2 * (parity & 1)).astype(jnp.float32).astype(jnp.bfloat16)
+
+
+def scale_of(largest):
+    scale = jnp.full_like(largest, 2.0**-8)
+    inv = jnp.full_like(largest, 2.0**8)
+    for e in (32, 16, 8, 4, 2, 1):
+        cand = scale * 2.0**e
+        take = largest > cand * 63.5
+        scale = jnp.where(take, cand, scale)
+        inv = jnp.where(take, inv * 2.0**-e, inv)
+    return jnp.minimum(scale, 2.0**30), jnp.maximum(inv, 2.0**-30)
+
+
+def inverse_of(power):
+    scale = jnp.full_like(power, 2.0**-8)
+    inv = jnp.full_like(power, 2.0**8)
+    for e in (32, 16, 8, 4, 2, 1):
+        cand = scale * 2.0**e
+        take = power >= cand
+        scale = jnp.where(take, cand, scale)
+        inv = jnp.where(take, inv * 2.0**-e, inv)
+    return inv
+
+
+def merge_meta(a, b):
+    row = lax.broadcasted_iota(jnp.int32, a.shape, 0)
+    return jnp.where(row < 2, jnp.minimum(a, b), a + b)
+
+
+def wire_meta(m):
+    unit, total = m[0:2], m[2:4]
+    inv = inverse_of(unit)
+    exact = total * inv * 127.0 <= 32767.0
+    nan = jnp.full_like(unit, jnp.nan)
+    zero = jnp.zeros((4, BLOCK), jnp.float32)
+    return inv, jnp.concatenate([jnp.where(exact, unit, nan), jnp.where(exact, total, nan), zero], axis=0)
+
+
+def kernel(
+    x_ref, cot_ref, sb_ref, rot_ref, mean_ref,
+    ct3, tmp, own, out_, got, om, sm, gm, acc, accm,
+    zs, zsm, zr, zrm, xs, xsm, xr, xrm, gbuf, parts, mblk,
+    sib_s, sib_r, z_s, z_r, x_s, x_r, g_s, g_r, a_s, a_r, f_s, f_r, l_s,
+):
+    g = lax.axis_index("group")
+    d = lax.axis_index("dev")
+    xl, y = g // 4, g % 4
+    xh, z, c = d // 8, (d // 2) % 4, d % 2
+    z_hi, k = z // 2, (z % 2) * 2 + c
+    x = xh * 2 + xl
+
+    def dev(xx, yy, zz, cc):
+        return ((xx % 2) * 4 + yy, (xx // 2) * 8 + zz * 2 + cc)
+
+    sibling = dev(x, y, z, 1 - c)
+    partner = dev((x + 2) % 4, y, z, c)
+    self_send = (k == g // 2).astype(jnp.int32)
+
+    bar = pltpu.get_barrier_semaphore()
+
+    def greet(who):
+        pl.semaphore_signal(bar, inc=1, device_id=who, device_id_type=MESH)
+
+    greet(sibling)
+    for delta in (1, 2, 3):
+        greet(dev((x + delta) % 4, y, z, c))
+        greet(dev(x, (y + delta) % 4, z, c))
+        greet(dev(x, y, (z + delta) % 4, c))
+    ksrc = g // 2
+    zsrc, csrc = z_hi * 2 + ksrc // 2, ksrc % 2
+    for other in range(8):
+
+        @pl.when(jnp.logical_or(self_send == 0, g != other))
+        def _():
+            greet((jnp.int32(other), xh * 8 + zsrc * 2 + csrc))
+
+    hmat = hadamard_in_kernel()
+    signs = (2 * sb_ref[...] - 1).astype(jnp.float32)
+    for blk in range(8):
+        cols = slice(blk * BLOCK, (blk + 1) * BLOCK)
+        signed = (cot_ref[:, cols].astype(jnp.float32) * signs[:, cols]).astype(jnp.bfloat16)
+        turned = lax.dot_general(hmat, signed, (((1,), (1,)), ((), ())), preferred_element_type=jnp.float32)
+        hi = turned.astype(jnp.bfloat16)
+        rest = turned - hi.astype(jnp.float32)
+        mid = rest.astype(jnp.bfloat16)
+        low = (rest - mid.astype(jnp.float32)).astype(jnp.bfloat16)
+        kk, b = blk // 2, blk % 2
+        r0 = (kk % 2) * 512 + (kk // 2) * 256 + b * BLOCK
+        rows = slice(r0, r0 + BLOCK)
+        for n, term in enumerate((hi, mid, low)):
+            ct3[rows, n * 256 : (n + 1) * 256] = term[:, :256]
+        ct3[rows, 768:896] = jnp.concatenate([hi[:, 256:], mid[:, 256:]], axis=1)
+        ct3[rows, 896:1024] = jnp.concatenate([low[:, 256:], jnp.zeros((BLOCK, 64), jnp.bfloat16)], axis=1)
+
+    def compute(s, core, lev, met):
+        for X in (0, 1):
+            lanes = [pl.ds(pl.multiple_of(X * 2304 + h * QUAD + s * BLOCK, BLOCK), BLOCK) for h in (0, 1)]
+            xa = jnp.concatenate([x_ref[:, l] for l in lanes], axis=1)
+            x3 = jnp.concatenate([xa[:256]] * 3 + [xa[256:]] * 3 + [jnp.zeros((64, 256), jnp.bfloat16)], axis=0)
+            lhs = ct3[pl.ds(pl.multiple_of(core * 512, 512), 512), :]
+            tmp[...] = jnp.dot(lhs, x3, preferred_element_type=jnp.float32)
+
+            def sub(Z, b):
+                return tmp[(Z % 2) * 256 + b * BLOCK : (Z % 2) * 256 + (b + 1) * BLOCK, (Z // 2) * BLOCK : (Z // 2 + 1) * BLOCK]
+
+            largest = jnp.concatenate(
+                [jnp.max(jnp.abs(sub(Z, b)), axis=0, keepdims=True) for Z in range(4) for b in range(2)], axis=0
+            )
+            scale, inv = scale_of(largest)
+            for Z in range(4):
+                for b in range(2):
+                    r = Z * 2 + b
+                    level = (sub(Z, b) * inv[r : r + 1] + MAGIC) - MAGIC
+                    lev[s, X, Z, b * BLOCK : (b + 1) * BLOCK, :] = (level * scale[r : r + 1]).astype(jnp.bfloat16)
+                mine = scale[2 * Z : 2 * Z + 2]
+                met[s, X, Z] = jnp.concatenate([mine, mine, jnp.zeros((4, BLOCK), jnp.float32)], axis=0)
+
+    def remote(src, dst, ss, rs, who):
+        return pltpu.make_async_remote_copy(src, dst, ss, rs, device_id=who, device_id_type=MESH)
+
+    def sib_copies(s):
+        return (
+            remote(out_.at[s], got.at[s], sib_s.at[s, 0], sib_r.at[s, 0], sibling),
+            remote(sm.at[s], gm.at[s], sib_s.at[s, 1], sib_r.at[s, 1], sibling),
+        )
+
+    def z_copies_zfirst(s, dz):
+        who = dev(x, y, (z + dz) % 4, c)
+        i = dz - 1
+        return (
+            remote(zs.at[s, i], zr.at[s, i], z_s.at[s, i, 0], z_r.at[s, i, 0], who),
+            remote(zsm.at[s, i], zrm.at[s, i], z_s.at[s, i, 1], z_r.at[s, i, 1], who),
+        )
+
+    def z_copies_xfirst(s, dz):
+        who = dev(x, y, (z + dz) % 4, c)
+        i = dz - 1
+        return (
+            remote(zs.at[s, i, 0], zr.at[s, i, 0], z_s.at[s, i, 0], z_r.at[s, i, 0], who),
+            remote(zsm.at[s, i, 0], zrm.at[s, i, 0], z_s.at[s, i, 1], z_r.at[s, i, 1], who),
+        )
+
+    def x_copies_zfirst(s):
+        return (
+            remote(xs.at[s, 0], xr.at[s, 0], x_s.at[s, 0], x_r.at[s, 0], partner),
+            remote(xsm.at[s, 0], xrm.at[s, 0], x_s.at[s, 1], x_r.at[s, 1], partner),
+        )
+
+    def x_copies_xfirst(s):
+        return (
+            remote(xs.at[s], xr.at[s], x_s.at[s, 0], x_r.at[s, 0], partner),
+            remote(xsm.at[s], xrm.at[s], x_s.at[s, 1], x_r.at[s, 1], partner),
+        )
+
+    def g_copies(j, b):
+        who = (2 * k + b, xh * 8 + (z_hi * 2 + j // 2) * 2 + j % 2)
+        src = gbuf.at[b, pl.ds(pl.multiple_of(j * OWN, 32), OWN), :]
+        return remote(src, parts.at[g], g_s.at[j, b], g_r.at[g], who)
+
+    def start(copies):
+        for copy in copies:
+            copy.start()
+
+    def arrive(copies):
+        for copy in copies:
+            copy.wait_recv()
+
+    def left(copies):
+        for copy in copies:
+            copy.wait_send()
+
+    def half(b):
+        return slice(b * BLOCK, (b + 1) * BLOCK)
+
+    def pair_block(s, X, Z, b):
+        return own[s, X, Z, half(b), :].astype(jnp.float32) + got[s, X, Z, half(b), :].astype(jnp.float32)
+
+    def encode(value, inv):
+        return (value * inv).astype(jnp.int16)
+
+    def decode(ref, index, b, meta):
+        return ref[index + (half(b), slice(None))].astype(jnp.float32) * meta[b : b + 1]
+
+    def pair(s):
+        arrive(sib_copies(s))
+
+        @pl.when(s % 2 == 1)
+        def _():
+            for X in (0, 1):
+                for b in (0, 1):
+                    acc[s, X, half(b), :] = pair_block(s, X, z, b)
+                accm[s, X] = merge_meta(om[s, X, z], gm[s, X, z])
+            for dz in (1, 2, 3):
+                Z = (z + dz) % 4
+                for X in (0, 1):
+                    inv, meta = wire_meta(merge_meta(om[s, X, Z], gm[s, X, Z]))
+                    zsm[s, dz - 1, X] = meta
+                    for b in (0, 1):
+                        zs[s, dz - 1, X, half(b), :] = encode(pair_block(s, X, Z, b), inv[b : b + 1])
+                start(z_copies_zfirst(s, dz))
+
+        @pl.when(s % 2 == 0)
+        def _():
+            for Z in range(4):
+                inv, meta = wire_meta(merge_meta(om[s, 1 - xh, Z], gm[s, 1 - xh, Z]))
+                xsm[s, Z] = meta
+                for b in (0, 1):
+                    xs[s, Z, half(b), :] = encode(pair_block(s, 1 - xh, Z, b), inv[b : b + 1])
+            start(x_copies_xfirst(s))
+            for Z in range(4):
+                for b in (0, 1):
+                    acc[s, Z, half(b), :] = pair_block(s, xh, Z, b)
+                accm[s, Z] = merge_meta(om[s, xh, Z], gm[s, xh, Z])
+
+    def second(s):
+        @pl.when(s % 2 == 1)
+        def _():
+            for dz in (1, 2, 3):
+                arrive(z_copies_zfirst(s, dz))
+            other = 1 - xh
+            metas = [zrm[s, i, other] for i in range(3)]
+            inv, meta = wire_meta(functools.reduce(merge_meta, metas, accm[s, other]))
+            xsm[s, 0] = meta
+            for b in (0, 1):
+                t = acc[s, other, half(b), :]
+                for i in range(3):
+                    t = t + decode(zr, (s, i, other), b, metas[i])
+                xs[s, 0, half(b), :] = encode(t, inv[b : b + 1])
+            start(x_copies_zfirst(s))
+            metas = [zrm[s, i, xh] for i in range(3)]
+            for b in (0, 1):
+                t = acc[s, xh, half(b), :]
+                for i in range(3):
+                    t = t + decode(zr, (s, i, xh), b, metas[i])
+                acc[s, xh, half(b), :] = t
+
+        @pl.when(s % 2 == 0)
+        def _():
+            arrive(x_copies_xfirst(s))
+            for dz in (1, 2, 3):
+                Z = (z + dz) % 4
+                arrived = xrm[s, Z]
+                inv, meta = wire_meta(merge_meta(accm[s, Z], arrived))
+                zsm[s, dz - 1, 0] = meta
+                for b in (0, 1):
+                    t = acc[s, Z, half(b), :] + decode(xr, (s, Z), b, arrived)
+                    zs[s, dz - 1, 0, half(b), :] = encode(t, inv[b : b + 1])
+                start(z_copies_xfirst(s, dz))
+            arrived = xrm[s, z]
+            for b in (0, 1):
+                acc[s, z, half(b), :] = acc[s, z, half(b), :] + decode(xr, (s, z), b, arrived)
+
+    def third(s):
+        @pl.when(s % 2 == 1)
+        def _():
+            arrive(x_copies_zfirst(s))
+            arrived = xrm[s, 0]
+            for b in (0, 1):
+                tmp[half(b), :BLOCK] = acc[s, xh, half(b), :] + decode(xr, (s, 0), b, arrived)
+
+        @pl.when(s % 2 == 0)
+        def _():
+            for dz in (1, 2, 3):
+                arrive(z_copies_xfirst(s, dz))
+            metas = [zrm[s, i, 0] for i in range(3)]
+            for b in (0, 1):
+                t = acc[s, z, half(b), :]
+                for i in range(3):
+                    t = t + decode(zr, (s, i, 0), b, metas[i])
+                tmp[half(b), :BLOCK] = t
+
+        largest = jnp.concatenate(
+            [jnp.max(jnp.abs(tmp[half(b), :BLOCK]), axis=0, keepdims=True) for b in (0, 1)], axis=0
+        )
+        scale, inv = scale_of(largest)
+        for b in (0, 1):
+            level = (tmp[half(b), :BLOCK] * inv[b : b + 1] + MAGIC) - MAGIC
+            value = level * scale[b : b + 1]
+            gbuf[b, pl.ds(pl.multiple_of(s * BLOCK, BLOCK), BLOCK), :] = value.T.astype(jnp.bfloat16)
+
+        @pl.when(jnp.logical_and(s >= 2, s % 2 == 0))
+        def _():
+            j = s // 2 - 1
+            for b in (0, 1):
+                to_self = jnp.logical_and(j == k, 2 * k + b == g)
+
+                @pl.when(to_self)
+                def _():
+                    parts[g] = gbuf[b, pl.ds(pl.multiple_of(j * OWN, 32), OWN), :]
+
+                @pl.when(jnp.logical_not(to_self))
+                def _():
+                    g_copies(j, b).start()
+
+    def first_loop(s, _):
+        @pl.when(s < STAGES)
+        def _():
+            compute(s, 1 - c, out_, sm)
+
+            @pl.when(s == 0)
+            def _():
+                pl.semaphore_wait(bar, 18 - self_send)
+
+            start(sib_copies(s))
+            compute(s, c, own, om)
+
+        @pl.when(s >= 1)
+        def _():
+            pair(s - 1)
+
+        return 0
+
+    lax.fori_loop(0, STAGES + 1, first_loop, 0)
+
+    LAG = 2
+
+    def second_loop(t, _):
+        @pl.when(t < STAGES)
+        def _():
+            second(t)
+
+        @pl.when(t >= LAG)
+        def _():
+            third(t - LAG)
+
+        return 0
+
+    lax.fori_loop(0, STAGES + LAG, second_loop, 0)
+
+    def await_part(other):
+        src = gbuf.at[0, pl.ds(0, OWN), :]
+
+        @pl.when(jnp.logical_or(self_send == 0, g != other))
+        def _():
+            remote(src, parts.at[other], g_s.at[0, 0], g_r.at[other], sibling).wait_recv()
+
+    await_part(0)
+    total = parts[0].astype(jnp.float32)
+    for other in range(1, 8):
+        await_part(other)
+        total = total + parts[other].astype(jnp.float32)
+        scale, inv = scale_of(jnp.max(jnp.abs(total), axis=1, keepdims=True))
+        total = ((total * inv + MAGIC) - MAGIC) * scale
+    total = total * (1.0 / 128.0)
+    rot_ref[...] = total.astype(jnp.bfloat16)
+    turned = jnp.dot(total.astype(jnp.bfloat16), hmat, preferred_element_type=jnp.float32)
+    my_signs = (2 * sb_ref[:, pl.ds(pl.multiple_of(g * BLOCK, BLOCK), BLOCK)] - 1).astype(jnp.float32)
+    mean = turned * (1.0 / BLOCK) * my_signs
+    bad = jnp.max(jnp.where(mean == mean, 0.0, 1.0), axis=(0, 1), keepdims=True)
+    mean = jnp.where(bad > 0.0, jnp.nan, mean)
+    mblk[...] = mean.astype(jnp.bfloat16)
+
+    order = ("xyz", "yzx", "zxy")
+
+    def rows(p):
+        return pl.ds(p * PART, PART)
+
+    def slabs(p, phase, xx, yy, zz):
+        hh, ll = xx // 2, xx % 2
+        if phase == 0:
+            cols = pl.ds(pl.multiple_of((ll * 4 + yy) * BLOCK, BLOCK), BLOCK)
+            return [mean_ref.at[hh, zz, c, rows(p), cols]]
+        quarter = [pl.ds(pl.multiple_of(l * 512 + yy * BLOCK, BLOCK), BLOCK) for l in (0, 1)]
+        whole_l = pl.ds(pl.multiple_of(ll * 512, 512), 512)
+        if p == 0:
+            if phase == 1:
+                return [mean_ref.at[:, zz, c, rows(p), q] for q in quarter]
+            return [mean_ref.at[:, zz, c, rows(p), :]]
+        if p == 1:
+            if phase == 1:
+                return [mean_ref.at[hh, zz, c, rows(p), whole_l]]
+            return [mean_ref.at[hh, :, c, rows(p), whole_l]]
+        if phase == 1:
+            cols = pl.ds(pl.multiple_of((ll * 4 + yy) * BLOCK, BLOCK), BLOCK)
+            return [mean_ref.at[hh, :, c, rows(p), cols]]
+        return [mean_ref.at[:, :, c, rows(p), q] for q in quarter]
+
+    def moved(axis, delta):
+        return (
+            (x + delta) % 4 if axis == "x" else x,
+            (y + delta) % 4 if axis == "y" else y,
+            (z + delta) % 4 if axis == "z" else z,
+        )
+
+    def gather_sends(p, phase, delta):
+        to = moved(order[p][phase], delta)
+        mine = slabs(p, phase, x, y, z)
+        src = [mblk.at[rows(p), :]] if phase == 0 else mine
+        return [
+            remote(a, b, a_s.at[p, phase, delta - 1, i], a_r.at[p, phase, delta - 1, i], dev(*to, c))
+            for i, (a, b) in enumerate(zip(src, mine))
+        ]
+
+    def gather_gets(p, phase, delta):
+        at = moved(order[p][phase], 4 - delta)
+        return [
+            remote(a, a, a_s.at[p, phase, delta - 1, i], a_r.at[p, phase, delta - 1, i], sibling)
+            for i, a in enumerate(slabs(p, phase, *at))
+        ]
+
+    def forwards(p, n):
+        at = (x, y, z) if n == 0 else moved(order[p][2], 4 - n)
+        return [
+            remote(a, a, f_s.at[p, n, i], f_r.at[p, n, i], sibling) for i, a in enumerate(slabs(p, 2, *at))
+        ]
+
+    def forwarded(p, n):
+        at = (x, y, z) if n == 0 else moved(order[p][2], 4 - n)
+        out = []
+        hh, ll = at[0] // 2, at[0] % 2
+        quarter = [pl.ds(pl.multiple_of(l * 512 + at[1] * BLOCK, BLOCK), BLOCK) for l in (0, 1)]
+        whole_l = pl.ds(pl.multiple_of(ll * 512, 512), 512)
+        if p == 0:
+            refs = [mean_ref.at[:, at[2], 1 - c, rows(p), :]]
+        elif p == 1:
+            refs = [mean_ref.at[hh, :, 1 - c, rows(p), whole_l]]
+        else:
+            refs = [mean_ref.at[:, :, 1 - c, rows(p), q] for q in quarter]
+        for i, a in enumerate(refs):
+            out.append(remote(a, a, f_s.at[p, n, i], f_r.at[p, n, i], sibling))
+        return out
+
+    home = mean_ref.at[xh, z, c, :, pl.ds(pl.multiple_of(g * BLOCK, BLOCK), BLOCK)]
+    keep = pltpu.make_async_copy(mblk, home, l_s)
+    keep.start()
+    for p in range(3):
+        for delta in (1, 3, 2):
+            start(gather_sends(p, 0, delta))
+    keep.wait()
+    for phase in (1, 2):
+        for p in range(3):
+            for delta in (1, 3, 2):
+                arrive(gather_gets(p, phase - 1, delta))
+            for delta in (1, 3, 2):
+                start(gather_sends(p, phase, delta))
+            if phase == 2:
+                start(forwards(p, 0))
+    for delta in (1, 3, 2):
+        for p in range(3):
+            arrive(gather_gets(p, 2, delta))
+            start(forwards(p, delta))
+
+    for p in range(3):
+        for n in (0, 1, 3, 2):
+            arrive(forwarded(p, n))
+    for p in range(3):
+        for n in range(4):
+            left(forwards(p, n))
+        for phase in range(3):
+            for delta in (1, 2, 3):
+                left(gather_sends(p, phase, delta))
+
+    def drain(s, _):
+        left(sib_copies(s))
+
+        @pl.when(s % 2 == 1)
+        def _():
+            for dz in (1, 2, 3):
+                left(z_copies_zfirst(s, dz))
+            left(x_copies_zfirst(s))
+
+        @pl.when(s % 2 == 0)
+        def _():
+            for dz in (1, 2, 3):
+                left(z_copies_xfirst(s, dz))
+            left(x_copies_xfirst(s))
+
+        return 0
+
+    lax.fori_loop(0, STAGES, drain, 0)
+
+    def drain_g(j, _):
+        for b in (0, 1):
+
+            @pl.when(jnp.logical_not(jnp.logical_and(j == k, 2 * k + b == g)))
+            def _():
+                g_copies(j, b).wait_send()
+
+        return 0
+
+    lax.fori_loop(0, 4, drain_g, 0)
+
+
+def fast(x_act, cotangent, sign_bits):
+    bf16, f32, i16 = jnp.bfloat16, jnp.float32, jnp.int16
+    dma = pltpu.SemaphoreType.DMA
+    vmem = pltpu.VMEM
+    rotated, mean = pl.pallas_call(
+        kernel,
+        out_shape=(
+            jax.ShapeDtypeStruct((OWN, BLOCK), bf16),
+            jax.ShapeDtypeStruct((2, 4, 2, OWN, KVW), bf16),
+        ),
+        in_specs=[pl.BlockSpec(memory_space=vmem)] * 3,
+        out_specs=(pl.BlockSpec(memory_space=vmem), pl.BlockSpec(memory_space=pl.ANY)),
+        scratch_shapes=[
+            vmem((KVW, KVW), bf16),
+            vmem((512, 256), f32),
+            vmem((STAGES, 2, 4, 256, BLOCK), bf16),
+            vmem((STAGES, 2, 4, 256, BLOCK), bf16),
+            vmem((STAGES, 2, 4, 256, BLOCK), bf16),
+            vmem((STAGES, 2, 4, 8, BLOCK), f32),
+            vmem((STAGES, 2, 4, 8, BLOCK), f32),
+            vmem((STAGES, 2, 4, 8, BLOCK), f32),
+            vmem((STAGES, 4, 256, BLOCK), f32),
+            vmem((STAGES, 4, 8, BLOCK), f32),
+            vmem((STAGES, 3, 2, 256, BLOCK), i16),
+            vmem((STAGES, 3, 2, 8, BLOCK), f32),
+            vmem((STAGES, 3, 2, 256, BLOCK), i16),
+            vmem((STAGES, 3, 2, 8, BLOCK), f32),
+            vmem((STAGES, 4, 256, BLOCK), i16),
+            vmem((STAGES, 4, 8, BLOCK), f32),
+            vmem((STAGES, 4, 256, BLOCK), i16),
+            vmem((STAGES, 4, 8, BLOCK), f32),
+            vmem((2, QUAD, BLOCK), bf16),
+            vmem((8, OWN, BLOCK), bf16),
+            vmem((OWN, BLOCK), bf16),
+            dma((STAGES, 2)), dma((STAGES, 2)),
+            dma((STAGES, 3, 2)), dma((STAGES, 3, 2)),
+            dma((STAGES, 2)), dma((STAGES, 2)),
+            dma((4, 2)), dma((8,)),
+            dma((3, 3, 3, 2)), dma((3, 3, 3, 2)),
+            dma((3, 4, 2)), dma((3, 4, 2)),
+            dma,
+        ],
+        compiler_params=pltpu.CompilerParams(
+            collective_id=0, has_side_effects=True, vmem_limit_bytes=60 * 2**20
+        ),
+        cost_estimate=pl.CostEstimate(flops=10**10, bytes_accessed=3 * 10**7, transcendentals=0),
+        name="sync",
+    )(x_act, cotangent, sign_bits.reshape(1, KVW))
+    return rotated, mean
 
 
 def passed_along(value, axis, steps):
@@ -62,7 +617,7 @@
     return (blocks * scales.astype(jnp.float32)[..., None]).reshape(shape)
 
 
-def body(x_act, cotangent, sign_bits):
+def general(x_act, cotangent, sign_bits):
     signs = (2 * sign_bits - 1).astype(jnp.float32)
     hmat = hadamard()
     local = lax.dot_general(
@@ -110,6 +665,19 @@
     return (rotated_sum, mean_grad)
 
 
+def body(x_act, cotangent, sign_bits):
+    rotated, mean = fast(x_act, cotangent, sign_bits)
+    marks = mean[:, :, :, 0, ::BLOCK].astype(jnp.float32)
+    inexact = jnp.any(marks != marks)
+    return lax.cond(
+        inexact,
+        lambda r, m: general(x_act, cotangent, sign_bits),
+        lambda r, m: (r, m),
+        rotated,
+        mean.reshape(D, KVW),
+    )
+
+
 def solution(mesh):
     placed = (P(("group", "dev"), None), P(("group", "dev"), None), P())
     return jax.shard_map(

time: 670 us -> 143 us (0.21)
  waiting for transfers between devices: 276 us -> 0 us
  Pallas kernels: 0 us -> 114 us
  local copies, waits for them, and re-layouts: 105 us -> 12.7 us
  other arithmetic: 83.8 us -> 0.65 us
  starting transfers between devices: 78.8 us -> 0 us
  matrix products: 58.4 us -> 0 us
  blocking collectives: 49.2 us -> 0 us
    pallas_call x0 -> x1, Pallas kernels: none -> 114 us  [fast(): pl.pallas_call(kernel, out_shape=(jax.ShapeDtypeStruct((OWN, BLOCK), bf16...]
    all_to_all x2 -> x0, waiting for transfers between devices: 108 us -> none  [the longest x1 108 us: body(): lax.all_to_all(levels.reshape(members, rows, width), 'dev', split_axis=0,...]
    psum x1 -> x0, waiting for transfers between devices: 99.9 us -> none  [from_root(): return lax.psum(jnp.where(mine, x, jnp.zeros_like(x)), axis)]
    ppermute x14 -> x0, starting transfers between devices: 62.2 us -> none  [passed_along(): lax.ppermute(value, axis, [(source, source + steps) for source in range(l...]
    dot_general x3 -> x0, matrix products: 58.4 us -> none  [the longest x1 28.6 us: unrotate(): jnp.einsum('rbi,ij->rbj', blocks, hmat, precision=lax.Precision.HIGHEST)]
    mul x18 -> x0, local copies, waits for them, and re-layouts: 46.3 us -> none  [dequant(): return (blocks * scales.astype(jnp.float32)[..., None]).reshape(shape)]
    ppermute x14 -> x0, waiting for transfers between devices: 35.7 us -> none  [passed_along(): lax.ppermute(value, axis, [(source, source + steps) for source in range(l...]
    all_gather x1 -> x0, blocking collectives: 35.1 us -> none  [body(): lax.all_gather(final[1], 'dev', axis=0, tiled=True)]
  transfers between devices with their start and end apart: 18 -> 0, of which waited for: 10 -> 0; matrix products, arithmetic and copies ran while one was open for 11% -> 0% of each run, Pallas kernels for 0% -> 0%
where the time goes in v1:
time: 143 us; the launch traced here: 142 us
  Pallas kernels  114 us (80%)
  between operations  14.7 us (10%)
  local copies, waits for them, and re-layouts  12.7 us (9%)
    pallas_call x1, Pallas kernels, fast(): pl.pallas_call(kernel, out_shape=(jax.ShapeDtypeStruct((OWN, BLOCK), bf16...  114 us
    unnamed x6, local copies, waits for them, and re-layouts  9.18 us
    slice x1, local copies, waits for them, and re-layouts, body(): marks = mean[:, :, :, 0, ::BLOCK].astype(jnp.float32)  3.54 us

profile of v1, /device:TPU:1, one launch (start us, length us, event | category | flops | bytes accessed | tf_op | source)
XLA Modules:
  0.0 142.4 jit_solution(16395335297711873392)
XLA Ops:
  7.2 0.0 copy-start.3
  7.2 0.0 copy-start.7
  7.2 114.1 %sync.1 = (bf16[288,128]{1,0:T(8,128)(2,1)S(1)}, bf16[2,4,2,288,1024]{4,3,2,1,0:T(8,128)(2,1)}) custom-call(bf16[320,4608]{1,0:T(8,128)(2,1)} %x_ref.1, bf16[320,1024]{1,0:T(8,128)(2,1)} %cot_ref.1, s32[1,1024]{1,0:T(1,128)} %bitcast.115), custom_call_target="tpu_custom_call" | custom-call | flops 10000000000 | bytes 30000000 | tf_op jit(solution)/shard_map/sync/pallas_call | solution.py:517
  121.3 3.5 %slice.3 = bf16[2,4,2,1,8]{4,3,2,1,0:T(2,128)(2,1)S(1)} slice(bf16[2,4,2,288,1024]{4,3,2,1,0:T(8,128)(2,1)} %get-tuple-element.304), slice={[0:2:1], [0:4:1], [0:2:1], [0:1:1], [0:1024:128]} | slice | bytes 512 | tf_op jit(solution)/shard_map/slice | solution.py:670
  124.8 0.7 compare_reduce_fusion
  126.1 0.0 copy-done.3
  126.1 0.0 copy-done.7
  126.2 0.2 conditional.1
  126.4 0.6 copy.149
  127.0 8.5 %copy.150 = bf16[4608,1024]{1,0:T(8,128)(2,1)} copy(bf16[4608,1024]{1,0:T(8,128)(2,1)} %get-tuple-element.309) | data formatting | bytes 18874368
Async XLA Ops:
  7.2 119.0 %copy-start.3 = (bf16[320,4608]{1,0:T(8,128)(2,1)S(1)}, bf16[320,4608]{1,0:T(8,128)(2,1)}, u32[]{:S(2)}) copy-start(bf16[320,4608]{1,0:T(8,128)(2,1)} %x_ref.1) | copy-start | bytes 8847364
  7.2 119.0 %copy-start.7 = (s32[1024]{0:T(1024)S(1)}, s32[1024]{0:T(1024)}, u32[]{:S(2)}) copy-start(s32[1024]{0:T(1024)} %param.12) | copy-start | bytes 12292

commit v2 on v0

--- a/solution.py
+++ b/solution.py
@@ -1,20 +1,624 @@
+import functools
+
 import jax
 import jax.numpy as jnp
 from jax import lax
+from jax.experimental import pallas as pl
+from jax.experimental.pallas import tpu as pltpu
 from jax.sharding import PartitionSpec as P
 
 BLOCK = 128
-
-
-def passed_along(value, axis, steps):
-    count = lax.axis_size(axis)
-    leading, last = (max(0, -steps), min(count, count - steps))
-    return lax.ppermute(value, axis, [(source, source + steps) for source in range(leading, last)])
-
-
-def from_root(x, axis, root):
-    mine = lax.axis_index(axis) == root
-    return lax.psum(jnp.where(mine, x, jnp.zeros_like(x)), axis)
+TOK = 320
+D = 4608
+KVW = 1024
+STAGES = 9
+QUAD = 1152
+OWN = 288
+PART = 96
+SHARE = 32
+LAG_A, LAG_B, LAG_C, LAG_D = 1, 5, 8, 10
+MAGIC = 12582912.0
+MESH = pl.DeviceIdType.MESH
+
+
+def hadamard_in_kernel():
+    i = lax.broadcasted_iota(jnp.int32, (BLOCK, BLOCK), 0)
+    j = lax.broadcasted_iota(jnp.int32, (BLOCK, BLOCK), 1)
+    both = i & j
+    parity = jnp.zeros_like(both)
+    for bit in range(7):
+        parity = parity + ((both >> bit) & 1)
+    return (1 - 2 * (parity & 1)).astype(jnp.float32).astype(jnp.bfloat16)
+
+
+def scale_of(largest):
+    scale = jnp.full_like(largest, 2.0**-8)
+    for e in (32, 16, 8, 4, 2, 1):
+        cand = scale * 2.0**e
+        scale = jnp.where(largest > cand * 63.5, cand, scale)
+    return jnp.minimum(scale, 2.0**30)
+
+
+def rounded(value, scale):
+    shift = scale * MAGIC
+    return (value + shift) - shift
+
+
+def inverse_of(power):
+    scale = jnp.full_like(power, 2.0**-8)
+    inv = jnp.full_like(power, 2.0**8)
+    for e in (32, 16, 8, 4, 2, 1):
+        cand = scale * 2.0**e
+        take = power >= cand
+        scale = jnp.where(take, cand, scale)
+        inv = jnp.where(take, inv * 2.0**-e, inv)
+    return inv
+
+
+def on_wire(unit, total):
+    inv = inverse_of(unit)
+    exact = total * inv * 127.0 <= 32767.0
+    return inv, jnp.where(exact, unit, jnp.nan), jnp.where(exact, total, jnp.nan)
+
+
+def kernel(
+    x_hbm, cot_ref, sb_ref, rot_ref, gat, bad_ref,
+    xv, ct3, tmp0, tmp1, tmp2, tmp3, own, out_, got, om, sm, gm, pw, acc, accm,
+    z1, z1m, z1r, z1rm, z2, z2m, z2r, z2rm, xs, xsm, xr, xrm, gbuf, parts, rbuf, rgot, gauge,
+    sib_s, sib_r, z1_s, z1_r, z2_s, z2_r, x_s, x_r, g_s, g_r, r_s, r_r, a_s, a_r, f_r, l_s,
+):
+    g = lax.axis_index("group")
+    d = lax.axis_index("dev")
+    div, rem = (lambda a, b: lax.div(a, jnp.int32(b))), (lambda a, b: lax.rem(a, jnp.int32(b)))
+    xl, y = div(g, 4), rem(g, 4)
+    xh, z, c = div(d, 8), rem(div(d, 2), 4), rem(d, 2)
+    z_hi, k = div(z, 2), rem(z, 2) * 2 + c
+    x = xh * 2 + xl
+
+    def dev(xx, yy, zz, cc):
+        return (rem(xx, 2) * 4 + yy, div(xx, 2) * 8 + zz * 2 + cc)
+
+    sibling = dev(x, y, z, 1 - c)
+    partner = dev((x + 2) % 4, y, z, c)
+    beside = (dev(x, y, (z + 1) % 4, c), dev(x, y, (z + 3) % 4, c))
+    column = 2 * k + g // 4
+    to_self = jnp.logical_and(k == g // 2, g % 2 == g // 4).astype(jnp.int32)
+
+    fetch = pltpu.make_async_copy(x_hbm, xv, l_s)
+    fetch.start()
+
+    bar = pltpu.get_barrier_semaphore()
+
+    def greet(who):
+        pl.semaphore_signal(bar, inc=1, device_id=who, device_id_type=MESH)
+
+    greet(sibling)
+    for delta in (1, 2, 3):
+        greet(dev((x + delta) % 4, y, z, c))
+        greet(dev(x, (y + delta) % 4, z, c))
+        greet(dev(x, y, (z + delta) % 4, c))
+    for delta in (1, 2, 3):
+        greet(dev(xh * 2 + 1 - xl, (y + delta) % 4, z, c))
+    ksrc = g // 2
+    for m in range(4):
+
+        @pl.when(jnp.logical_or(to_self == 0, m != g % 4))
+        def _():
+            greet(((g % 2) * 4 + m, xh * 8 + (z_hi * 2 + ksrc // 2) * 2 + ksrc % 2))
+
+    hmat = hadamard_in_kernel()
+    signs = (2 * sb_ref[...] - 1).astype(jnp.float32)
+    for blk in range(8):
+        cols = slice(blk * BLOCK, (blk + 1) * BLOCK)
+        signed = (cot_ref[:, cols].astype(jnp.float32) * signs[:, cols]).astype(jnp.bfloat16)
+        turned = lax.dot_general(hmat, signed, (((1,), (1,)), ((), ())), preferred_element_type=jnp.float32)
+        hi = turned.astype(jnp.bfloat16)
+        rest = turned - hi.astype(jnp.float32)
+        mid = rest.astype(jnp.bfloat16)
+        low = (rest - mid.astype(jnp.float32)).astype(jnp.bfloat16)
+        kk, b = blk // 2, blk % 2
+        r0 = (kk % 2) * 512 + (kk // 2) * 256 + b * BLOCK
+        rows = slice(r0, r0 + BLOCK)
+        for n, term in enumerate((hi, mid, low)):
+            ct3[rows, n * 256 : (n + 1) * 256] = term[:, :256]
+        ct3[rows, 768:896] = jnp.concatenate([hi[:, 256:], mid[:, 256:]], axis=1)
+        ct3[rows, 896:1024] = jnp.concatenate([low[:, 256:], jnp.zeros((BLOCK, 64), jnp.bfloat16)], axis=1)
+
+    def product(s, core, X, tmp):
+        lanes = [pl.ds(pl.multiple_of(X * 2304 + h * QUAD + s * BLOCK, BLOCK), BLOCK) for h in (0, 1)]
+        xa = jnp.concatenate([xv[:, l] for l in lanes], axis=1)
+        x3 = jnp.concatenate([xa[:256]] * 3 + [xa[256:]] * 3 + [jnp.zeros((64, 256), jnp.bfloat16)], axis=0)
+        lhs = ct3[pl.ds(pl.multiple_of(core * 512, 512), 512), :]
+        tmp[...] = jnp.dot(lhs, x3, preferred_element_type=jnp.float32)
+
+    def quantized(s, X, tmp, lev, met):
+        def sub(Z, b):
+            r0, l0 = (Z % 2) * 256 + b * BLOCK, (Z // 2) * BLOCK
+            return tmp[r0 : r0 + BLOCK, l0 : l0 + BLOCK]
+
+        largest = jnp.concatenate(
+            [jnp.max(jnp.abs(sub(Z, b)), axis=0, keepdims=True) for Z in range(4) for b in range(2)], axis=0
+        )
+        scale = scale_of(largest)
+        met[s, X] = scale
+        for Z in range(4):
+            for b in range(2):
+                r = Z * 2 + b
+                lev[s, X, Z, half(b), :] = rounded(sub(Z, b), scale[r : r + 1]).astype(jnp.bfloat16)
+
+    def half(b):
+        return slice(b * BLOCK, (b + 1) * BLOCK)
+
+    def remote(src, dst, ss, rs, who):
+        return pltpu.make_async_remote_copy(src, dst, ss, rs, device_id=who, device_id_type=MESH)
+
+    def both(src, srcm, dst, dstm, ss, n, rs, who):
+        return (remote(src, dst, ss.at[2 * n], rs, who), remote(srcm, dstm, ss.at[2 * n + 1], rs, who))
+
+    def sib_copies(s):
+        return both(out_.at[s], sm.at[s], got.at[s], gm.at[s], sib_s, 0, sib_r.at[s], sibling)
+
+    def z1_copies(s, way, n):
+        a, b = z1.at[s, way], z1r.at[s, way]
+        if n == 1:
+            a, b = a.at[0], b.at[0]
+        return both(a, z1m.at[s, way], b, z1rm.at[s, way], z1_s, n - 1, z1_r.at[s, way], beside[way])
+
+    def z2_copies(s, way, n):
+        a, b = z2.at[s, way], z2r.at[s, way]
+        if n == 1:
+            a, b = a.at[0], b.at[0]
+        return both(a, z2m.at[s, way], b, z2rm.at[s, way], z2_s, n - 1, z2_r.at[s, way], beside[way])
+
+    def x_copies(s, n):
+        a, am, b, bm = xs.at[s], xsm.at[s], xr.at[s], xrm.at[s]
+        if n == 1:
+            a, am, b, bm = a.at[0], am.at[0], b.at[0], bm.at[0]
+        return both(a, am, b, bm, x_s, 0 if n == 1 else 1, x_r.at[s], partner)
+
+    def took(sem, rows):
+        ref = gauge.at[pl.ds(0, rows), :]
+        pltpu.make_async_copy(ref, ref, sem).wait()
+
+    def g_copy(p, q):
+        to = rem(g + q, 8)
+        three = pl.ds(pl.multiple_of(p * PART, PART), PART)
+        return remote(gbuf.at[to, three, :], parts.at[g, three, :], g_s, g_r.at[p], (to, d))
+
+    def r_copy(s):
+        t = 4 * s + rem(g, 4)
+        j = div(t, 9)
+        src = rbuf.at[pl.ds(pl.multiple_of(s * SHARE, SHARE), SHARE), :]
+        dst = rgot.at[pl.ds(pl.multiple_of(rem(t, 9) * SHARE, SHARE), SHARE), :]
+        who = (column, xh * 8 + (z_hi * 2 + div(j, 2)) * 2 + rem(j, 2))
+        return remote(src, dst, r_s.at[s], r_r.at[rem(t, 9)], who), jnp.logical_and(to_self == 1, j == k), t
+
+    def start(copies):
+        for copy in copies:
+            copy.start()
+
+    def encode(value, inv):
+        return (value * inv).astype(jnp.int16)
+
+    def pair_block(s, X, Z, b):
+        return own[s, X, Z, half(b), :].astype(jnp.float32) + got[s, X, Z, half(b), :].astype(jnp.float32)
+
+    def add(s, i, b, block, unit, total):
+        acc[s, i, half(b), :] = acc[s, i, half(b), :] + block.astype(jnp.float32) * unit
+        accm[s, i, b : b + 1, :] = jnp.minimum(accm[s, i, b : b + 1, :], unit)
+        accm[s, i, 2 + b : 3 + b, :] = accm[s, i, 2 + b : 3 + b, :] + total
+
+    def packed(s, i, b):
+        inv, unit, total = on_wire(accm[s, i, b : b + 1, :], accm[s, i, 2 + b : 3 + b, :])
+        return encode(acc[s, i, half(b), :], inv), unit, total
+
+    def z1_from_sums(s):
+        two = (z + 2) % 4
+        for way, (near, b) in enumerate((((z + 1) % 4, 1), ((z + 3) % 4, 0))):
+            for kind, (i, bb) in enumerate(((near, b), (two, 1 - b))):
+                block, unit, total = packed(s, i, bb)
+                z1[s, way, 0, kind] = block
+                z1m[s, way, kind : kind + 1, :] = unit
+                z1m[s, way, 2 + kind : 3 + kind, :] = total
+            start(z1_copies(s, way, 1))
+
+    def z1_take(s, n, mine, right, left_):
+        for way in (0, 1):
+            took(z1_r.at[s, way], 256 * n + 16)
+            for i in range(n):
+                r = 4 * i
+                b = way
+                on = right(i) if way == 0 else left_(i)
+                add(s, on, b, z1r[s, way, i, 1], z1rm[s, way, r + 1 : r + 2, :], z1rm[s, way, r + 3 : r + 4, :])
+                block, unit, total = packed(s, on, b)
+                z2[s, way, i] = block
+                z2m[s, way, i : i + 1, :] = unit
+                z2m[s, way, 2 + i : 3 + i, :] = total
+            start(z2_copies(s, way, n))
+            for i in range(n):
+                r = 4 * i
+                add(s, mine(i), 1 - way, z1r[s, way, i, 0], z1rm[s, way, r : r + 1, :], z1rm[s, way, r + 2 : r + 3, :])
+
+    def z2_take(s, n, mine):
+        for way in (0, 1):
+            took(z2_r.at[s, way], 128 * n + 16)
+            for i in range(n):
+                add(s, mine(i), way, z2r[s, way, i], z2rm[s, way, i : i + 1, :], z2rm[s, way, 2 + i : 3 + i, :])
+
+    def along_z_first(s):
+        return rem(s, 3) != 1
+
+    def step_a(s):
+        took(sib_r.at[s], 2080)
+        for X in (0, 1):
+            unit = jnp.minimum(om[s, X], gm[s, X])
+            total = om[s, X] + gm[s, X]
+            inv, wire_unit, wire_total = on_wire(unit, total)
+            for n, v in enumerate((unit, total, inv, wire_unit, wire_total)):
+                pw[X, n] = v
+
+        def row(X, n, Z, b):
+            return pw[X, n, pl.ds(2 * Z + b, 1), :]
+
+        def keep(i, ii, X, Z, b):
+            acc[s, i, half(ii), :] = pair_block(s, X, Z, b)
+            accm[s, i, ii : ii + 1, :] = row(X, 0, Z, b)
+            accm[s, i, 2 + ii : 3 + ii, :] = row(X, 1, Z, b)
+
+        @pl.when(along_z_first(s))
+        def _():
+            two, after, before = (z + 2) % 4, (z + 1) % 4, (z + 3) % 4
+            for way, (near, b) in enumerate(((after, 1), (before, 0))):
+                for X in (0, 1):
+                    for kind, (Z, bb) in enumerate(((near, b), (two, 1 - b))):
+                        z1[s, way, X, kind] = encode(pair_block(s, X, Z, bb), row(X, 2, Z, bb))
+                        z1m[s, way, 4 * X + kind : 4 * X + kind + 1, :] = row(X, 3, Z, bb)
+                        z1m[s, way, 4 * X + 2 + kind : 4 * X + 3 + kind, :] = row(X, 4, Z, bb)
+                start(z1_copies(s, way, 2))
+            for X in (0, 1):
+                for b in (0, 1):
+                    keep(X, b, X, z, b)
+                keep(2 + X, 0, X, after, 0)
+                keep(2 + X, 1, X, before, 1)
+
+        @pl.when(jnp.logical_not(along_z_first(s)))
+        def _():
+            for Z in range(4):
+                for b in (0, 1):
+                    xs[s, Z, half(b), :] = encode(pair_block(s, 1 - xh, Z, b), row(1 - xh, 2, Z, b))
+                    xsm[s, Z, b : b + 1, :] = row(1 - xh, 3, Z, b)
+                    xsm[s, Z, 2 + b : 3 + b, :] = row(1 - xh, 4, Z, b)
+            start(x_copies(s, 4))
+            for Z in range(4):
+                for b in (0, 1):
+                    keep(Z, b, xh, Z, b)
+
+    def x_take(s, i, n):
+        for b in (0, 1):
+            add(s, i, b, xr[s, n, half(b), :], xrm[s, n, b : b + 1, :], xrm[s, n, 2 + b : 3 + b, :])
+
+    def step_b(s):
+        @pl.when(along_z_first(s))
+        def _():
+            z1_take(s, 2, lambda i: i, lambda i: 2 + i, lambda i: 2 + i)
+
+        @pl.when(jnp.logical_not(along_z_first(s)))
+        def _():
+            took(x_r.at[s], 1088)
+            for Z in range(4):
+                x_take(s, Z, Z)
+            z1_from_sums(s)
+
+    def step_c(s):
+        @pl.when(along_z_first(s))
+        def _():
+            z2_take(s, 2, lambda i: i)
+            for b in (0, 1):
+                block, unit, total = packed(s, 1 - xh, b)
+                xs[s, 0, half(b), :] = block
+                xsm[s, 0, b : b + 1, :] = unit
+                xsm[s, 0, 2 + b : 3 + b, :] = total
+            start(x_copies(s, 1))
+
+        @pl.when(jnp.logical_not(along_z_first(s)))
+        def _():
+            z1_take(s, 1, lambda i: z, lambda i: (z + 1) % 4, lambda i: (z + 3) % 4)
+
+    def step_d(s):
+        @pl.when(along_z_first(s))
+        def _():
+            took(x_r.at[s], 272)
+            x_take(s, xh, 0)
+
+        @pl.when(jnp.logical_not(along_z_first(s)))
+        def _():
+            z2_take(s, 1, lambda i: z)
+
+        i = jnp.where(along_z_first(s), xh, z)
+        sums = [acc[s, i, half(b), :] for b in (0, 1)]
+        largest = jnp.concatenate([jnp.max(jnp.abs(t), axis=0, keepdims=True) for t in sums], axis=0)
+        scale = scale_of(largest)
+        for b in (0, 1):
+            value = rounded(sums[b], scale[b : b + 1])
+            value = value.T.astype(jnp.bfloat16)
+            for m in range(4):
+                gbuf[4 * b + m, pl.ds(pl.multiple_of(s * SHARE, SHARE), SHARE), :] = value[m * SHARE : (m + 1) * SHARE]
+
+        @pl.when(rem(s, 3) == 2)
+        def _():
+            for q in range(1, 8):
+                g_copy(div(s, 3), q).start()
+
+    fetch.wait()
+
+    def loop(t, _):
+        @pl.when(t < STAGES)
+        def _():
+            product(t, 1 - c, 0, tmp0)
+            product(t, 1 - c, 1, tmp1)
+            quantized(t, 0, tmp0, out_, sm)
+            product(t, c, 0, tmp2)
+            quantized(t, 1, tmp1, out_, sm)
+            product(t, c, 1, tmp3)
+
+            @pl.when(t == 0)
+            def _():
+                pl.semaphore_wait(bar, 17 - to_self)
+
+            start(sib_copies(t))
+            quantized(t, 0, tmp2, own, om)
+            quantized(t, 1, tmp3, own, om)
+
+        for lag, step in ((LAG_A, step_a), (LAG_B, step_b), (LAG_C, step_c), (LAG_D, step_d)):
+
+            @pl.when(jnp.logical_and(t >= lag, t < STAGES + lag))
+            def _():
+                step(t - lag)
+
+        return 0
+
+    lax.fori_loop(0, STAGES + LAG_D, loop, 0)
+
+    parts[g] = gbuf[g]
+    for p in range(3):
+        took(g_r.at[p], 7 * PART)
+    total = parts[0].astype(jnp.float32)
+    for other in range(1, 8):
+        total = total + parts[other].astype(jnp.float32)
+        total = rounded(total, scale_of(jnp.max(jnp.abs(total), axis=1, keepdims=True)))
+    total = total * (1.0 / 128.0)
+    rbuf[...] = total.astype(jnp.bfloat16)
+    turned = jnp.dot(total.astype(jnp.bfloat16), hmat, preferred_element_type=jnp.float32)
+    my_signs = (2 * sb_ref[:, pl.ds(pl.multiple_of(column * BLOCK, BLOCK), BLOCK)] - 1).astype(jnp.float32)
+    mean = turned * (1.0 / BLOCK) * my_signs
+    bad = jnp.max(jnp.where(mean == mean, 0.0, 1.0), axis=(0, 1), keepdims=True)
+    mean = jnp.where(bad > 0.0, jnp.nan, mean).astype(jnp.bfloat16)
+
+    order = ("xyz", "yzx", "zxy")
+
+    def moved(axis, delta):
+        return (
+            rem(x + delta, 4) if axis == "x" else x,
+            rem(y + delta, 4) if axis == "y" else y,
+            rem(z + delta, 4) if axis == "z" else z,
+        )
+
+    def at(p, core, where):
+        a = {"x": where[0], "y": where[1], "z": where[2]}
+        return (p, core, a[order[p][2]], a[order[p][1]], a[order[p][0]])
+
+    def to_mate(p, phase, delta, ref, n):
+        return remote(ref, ref, a_s.at[p, phase], a_r.at[p, n], dev(*moved(order[p][phase], delta), c))
+
+    def small(p, phase, delta):
+        return to_mate(p, phase, delta, gat.at[at(p, c, (x, y, z))[: 5 - phase]], phase)
+
+    def mine(p, n):
+        return {"x": x, "y": y, "z": z}[order[p][n]]
+
+    def half_slab(p, ring, h):
+        return gat.at[p, c, rem(mine(p, 2) + ring, 4), pl.ds(2 * h, 2)]
+
+    def last(p, way, h, ring, n):
+        return to_mate(p, 2, way, half_slab(p, ring, h), n)
+
+    def forward(p, ring):
+        ref = gat.at[p, c, rem(mine(p, 2) + ring, 4)]
+        return remote(ref, ref, a_s.at[p, 3], f_r.at[p], sibling)
+
+    for p in range(3):
+        gat[at(p, c, (x, y, z))] = mean[p * PART : (p + 1) * PART]
+        for delta in (1, 3, 2):
+            small(p, 0, delta).start()
+    for p in range(3):
+        took(a_r.at[p, 0], 3 * PART)
+        for delta in (1, 3, 2):
+            small(p, 1, delta).start()
+
+    def send_rotated(s, _):
+        copy, here, t = r_copy(s)
+
+        @pl.when(here)
+        def _():
+            rgot[pl.ds(pl.multiple_of(rem(t, 9) * SHARE, SHARE), SHARE), :] = rbuf[
+                pl.ds(pl.multiple_of(s * SHARE, SHARE), SHARE), :
+            ]
+
+        @pl.when(jnp.logical_not(here))
+        def _():
+            copy.start()
+
+        return 0
+
+    lax.fori_loop(0, STAGES, send_rotated, 0)
+
+    for ref, sem in (
+        (out_, sib_s.at[0]), (sm, sib_s.at[1]),
+        (z1.at[0:3, :, 0], z1_s.at[0]), (z1m.at[0:3], z1_s.at[1]), (z1.at[0:6], z1_s.at[2]), (z1m.at[0:6], z1_s.at[3]),
+        (z2.at[0:3, :, 0], z2_s.at[0]), (z2m.at[0:3], z2_s.at[1]), (z2.at[0:6], z2_s.at[2]), (z2m.at[0:6], z2_s.at[3]),
+        (xs.at[0:6, 0], x_s.at[0]), (xsm.at[0:6, 0], x_s.at[1]), (xs.at[0:3], x_s.at[2]), (xsm.at[0:3], x_s.at[3]),
+        (gbuf.at[0:7], g_s),
+    ):
+        pltpu.make_async_copy(ref, ref, sem).wait()
+    for p in range(3):
+        took(a_r.at[p, 1], 12 * PART)
+        last(p, 1, 0, 0, 2).start()
+        last(p, 3, 1, 0, 3).start()
+        last(p, 1, 1, 0, 4).start()
+        last(p, 3, 0, 0, 4).start()
+    for p in range(3):
+        forward(p, 0).start()
+    for p in range(3):
+        took(a_r.at[p, 2], 8 * PART)
+        last(p, 1, 0, 3, 5).start()
+        took(a_r.at[p, 3], 8 * PART)
+        last(p, 3, 1, 1, 5).start()
+    for p in range(3):
+        took(a_r.at[p, 4], 16 * PART)
+        forward(p, 3).start()
+        forward(p, 1).start()
+
+    def drain_rotated(u, _):
+        t = 9 * k + u
+
+        @pl.when(jnp.logical_or(to_self == 0, rem(t, 4) != rem(g, 4)))
+        def _():
+            ref = rgot.at[pl.ds(pl.multiple_of(u * SHARE, SHARE), SHARE), :]
+            remote(ref, ref, r_s.at[u], r_r.at[u], sibling).wait_recv()
+
+        copy, here, _ = r_copy(u)
+
+        @pl.when(jnp.logical_not(here))
+        def _():
+            copy.wait_send()
+
+        return 0
+
+    lax.fori_loop(0, STAGES, drain_rotated, 0)
+    rot_ref[...] = rgot[...]
+    for p in range(3):
+        took(a_r.at[p, 5], 16 * PART)
+        forward(p, 2).start()
+    for p in range(3):
+        took(f_r.at[p], 64 * PART)
+    for p in range(3):
+        for n, rows in enumerate((3, 12, 48, 64)):
+            took(a_s.at[p, n], rows * PART)
+    marks = jnp.zeros((16, BLOCK), jnp.float32)
+    for core in range(2):
+        for i in range(4):
+            for j in range(4):
+                for n in range(4):
+                    marks = marks + gat[0, core, i, j, n, 0:16, :].astype(jnp.float32)
+    bad_ref[0, 0] = jnp.max(jnp.where(marks == marks, 0.0, 1.0))
+
+
+def fast(x_act, cotangent, sign_bits):
+    bf16, f32, i16 = jnp.bfloat16, jnp.float32, jnp.int16
+    dma = pltpu.SemaphoreType.DMA
+    vmem = pltpu.VMEM
+    return pl.pallas_call(
+        kernel,
+        out_shape=(
+            jax.ShapeDtypeStruct((OWN, BLOCK), bf16),
+            vmem((3, 2, 4, 4, 4, PART, BLOCK), bf16),
+            jax.ShapeDtypeStruct((1, 1), f32),
+        ),
+        in_specs=[pl.BlockSpec(memory_space=pl.ANY)] + [pl.BlockSpec(memory_space=vmem)] * 2,
+        out_specs=(
+            pl.BlockSpec(memory_space=vmem),
+            pl.BlockSpec(memory_space=vmem),
+            pl.BlockSpec(memory_space=pltpu.SMEM),
+        ),
+        scratch_shapes=[
+            vmem((TOK, D), bf16),
+            vmem((KVW, KVW), bf16),
+            vmem((512, 256), f32), vmem((512, 256), f32), vmem((512, 256), f32), vmem((512, 256), f32),
+            vmem((STAGES, 2, 4, 256, BLOCK), bf16),
+            vmem((STAGES, 2, 4, 256, BLOCK), bf16),
+            vmem((STAGES, 2, 4, 256, BLOCK), bf16),
+            vmem((STAGES, 2, 8, BLOCK), f32),
+            vmem((STAGES, 2, 8, BLOCK), f32),
+            vmem((STAGES, 2, 8, BLOCK), f32),
+            vmem((2, 5, 8, BLOCK), f32),
+            vmem((STAGES, 4, 256, BLOCK), f32),
+            vmem((STAGES, 4, 8, BLOCK), f32),
+            vmem((STAGES, 2, 2, 2, BLOCK, BLOCK), i16),
+            vmem((STAGES, 2, 8, BLOCK), f32),
+            vmem((STAGES, 2, 2, 2, BLOCK, BLOCK), i16),
+            vmem((STAGES, 2, 8, BLOCK), f32),
+            vmem((STAGES, 2, 2, BLOCK, BLOCK), i16),
+            vmem((STAGES, 2, 8, BLOCK), f32),
+            vmem((STAGES, 2, 2, BLOCK, BLOCK), i16),
+            vmem((STAGES, 2, 8, BLOCK), f32),
+            vmem((STAGES, 4, 256, BLOCK), i16),
+            vmem((STAGES, 4, 8, BLOCK), f32),
+            vmem((STAGES, 4, 256, BLOCK), i16),
+            vmem((STAGES, 4, 8, BLOCK), f32),
+            vmem((8, OWN, BLOCK), bf16),
+            vmem((8, OWN, BLOCK), bf16),
+            vmem((OWN, BLOCK), bf16),
+            vmem((OWN, BLOCK), bf16),
+            vmem((64 * PART, BLOCK), bf16),
+            dma((2,)), dma((STAGES,)),
+            dma((4,)), dma((STAGES, 2)),
+            dma((4,)), dma((STAGES, 2)),
+            dma((4,)), dma((STAGES,)),
+            dma, dma((3,)),
+            dma((STAGES,)), dma((STAGES,)),
+            dma((3, 4)), dma((3, 6)),
+            dma((3,)), dma,
+        ],
+        compiler_params=pltpu.CompilerParams(
+            collective_id=0, has_side_effects=True, vmem_limit_bytes=47 * 2**20
+        ),
+        cost_estimate=pl.CostEstimate(flops=10**10, bytes_accessed=3 * 10**7, transcendentals=0),
+        name="sync",
+    )(x_act, cotangent, sign_bits.reshape(1, KVW))
+
+
+def assemble_kernel(gat, rot_ref, rot_out, out_hbm, rows, sems):
+    rot_out[...] = rot_ref[...]
+    copies = []
+    for quad in range(4):
+        for s in range(STAGES):
+            n = quad * STAGES + s
+            for k in range(4):
+                for g in range(8):
+                    xh, z, c = quad // 2, (quad % 2) * 2 + k // 2, k % 2
+                    x, y = xh * 2 + g // 4, g % 4
+                    p, r = s // 3, (s % 3) * SHARE
+                    where = ((z, y, x), (x, z, y), (y, x, z))[p]
+                    column = 2 * k + g // 4
+                    rows[
+                        n, y * SHARE : (y + 1) * SHARE, column * BLOCK : (column + 1) * BLOCK
+                    ] = gat[(p, c) + where + (slice(r, r + SHARE),)]
+            copies.append(
+                pltpu.make_async_copy(rows.at[n], out_hbm.at[pl.ds(n * BLOCK, BLOCK), :], sems.at[n])
+            )
+            copies[-1].start()
+    for copy in copies:
+        copy.wait()
+
+
+def assemble(gathered, rotated):
+    vmem = pl.BlockSpec(memory_space=pltpu.VMEM)
+    return pl.pallas_call(
+        assemble_kernel,
+        out_shape=(
+            jax.ShapeDtypeStruct((OWN, BLOCK), jnp.bfloat16),
+            jax.ShapeDtypeStruct((D, KVW), jnp.bfloat16),
+        ),
+        in_specs=[vmem, vmem],
+        out_specs=(vmem, pl.BlockSpec(memory_space=pl.ANY)),
+        scratch_shapes=[
+            pltpu.VMEM((4 * STAGES, BLOCK, KVW), jnp.bfloat16),
+            pltpu.SemaphoreType.DMA((4 * STAGES,)),
+        ],
+        compiler_params=pltpu.CompilerParams(vmem_limit_bytes=24 * 2**20),
+        cost_estimate=pl.CostEstimate(flops=0, bytes_accessed=2 * 10**7, transcendentals=0),
+        name="assemble",
+    )(gathered, rotated)
 
 
 def hadamard():
@@ -62,7 +666,7 @@
     return (blocks * scales.astype(jnp.float32)[..., None]).reshape(shape)
 
 
-def body(x_act, cotangent, sign_bits):
+def general(x_act, cotangent, sign_bits):
     signs = (2 * sign_bits - 1).astype(jnp.float32)
     hmat = hadamard()
     local = lax.dot_general(
@@ -86,28 +690,33 @@
         ),
     )
     group_total = jnp.sum(dequant(got_levels, got_scales), axis=0)
-    own = quantize(group_total)
+    part = dequant(*quantize(group_total)).astype(jnp.bfloat16)
+    blocks = part.reshape(rows, groups, BLOCK).swapaxes(0, 1)
+    arrived = lax.all_to_all(blocks, "group", split_axis=0, concat_axis=0, tiled=True).astype(jnp.float32)
+    running = arrived[0]
+    for other in range(1, groups):
+        running = dequant(*quantize(running + arrived[other]))
+    total = running / (groups * members)
     position = lax.axis_index("group")
-
-    def one_hop(step_idx, carry):
-        arrived = passed_along((carry[0], carry[1]), "group", 1)
-        merged = quantize(dequant(*arrived) + dequant(*own))
-        chosen = position == step_idx
-        return (jnp.where(chosen, merged[0], carry[0]), jnp.where(chosen, merged[1], carry[1]))
-
-    running = lax.fori_loop(1, groups, one_hop, own)
-    final = (from_root(running[0], "group", groups - 1), from_root(running[1], "group", groups - 1))
-    total = dequant(*final) / (groups * members)
-    column_share = width // groups
-    own_columns = lax.dynamic_slice_in_dim(total, position * column_share, column_share, 1)
-    rotated_sum = own_columns.astype(jnp.bfloat16)
-    all_levels, all_scales = (
-        lax.all_gather(final[0], "dev", axis=0, tiled=True),
-        lax.all_gather(final[1], "dev", axis=0, tiled=True),
+    my_signs = lax.dynamic_slice_in_dim(signs, position * BLOCK, BLOCK, 0)
+    mean = unrotate(total, my_signs, hmat).astype(jnp.bfloat16)
+    every = jnp.broadcast_to(mean[None], (groups, rows, BLOCK))
+    every = lax.all_to_all(every, "group", split_axis=0, concat_axis=0, tiled=True)
+    every = jnp.broadcast_to(every[None], (members, groups, rows, BLOCK))
+    every = lax.all_to_all(every, "dev", split_axis=0, concat_axis=0, tiled=True)
+    every = every.swapaxes(1, 2).reshape(members * rows, width)
+    return (total.astype(jnp.bfloat16), every)
+
+
+def body(x_act, cotangent, sign_bits):
+    rotated, gathered, inexact = fast(x_act, cotangent, sign_bits)
+    rotated, mean = assemble(gathered, rotated)
+    _, rotated, mean = lax.while_loop(
+        lambda state: state[0] > 0.0,
+        lambda state: (jnp.float32(0.0), *general(x_act, cotangent, sign_bits)),
+        (inexact[0, 0], rotated, mean),
     )
-    everything = dequant(all_levels, all_scales) / (groups * members)
-    mean_grad = unrotate(everything, signs, hmat).astype(jnp.bfloat16)
-    return (rotated_sum, mean_grad)
+    return rotated, mean
 
 
 def solution(mesh):

time: 670 us -> 95.2 us (0.14)
  waiting for transfers between devices: 276 us -> 0 us
  local copies, waits for them, and re-layouts: 105 us -> 0.9 us
  Pallas kernels: 0 us -> 92.4 us
  other arithmetic: 83.8 us -> 0 us
  starting transfers between devices: 78.8 us -> 0 us
  matrix products: 58.4 us -> 0 us
  blocking collectives: 49.2 us -> 0 us
  between operations: 14.2 us -> 0.87 us
    all_to_all x2 -> x0, waiting for transfers between devices: 108 us -> none  [the longest x1 108 us: body(): lax.all_to_all(levels.reshape(members, rows, width), 'dev', split_axis=0,...]
    psum x1 -> x0, waiting for transfers between devices: 99.9 us -> none  [from_root(): return lax.psum(jnp.where(mine, x, jnp.zeros_like(x)), axis)]
    pallas_call x0 -> x2, Pallas kernels: none -> 92.4 us  [the longest x1 87.9 us: fast(): pl.pallas_call(kernel, out_shape=(jax.ShapeDtypeStruct((OWN, BLOCK), bf16...]
    ppermute x14 -> x0, starting transfers between devices: 62.2 us -> none  [passed_along(): lax.ppermute(value, axis, [(source, source + steps) for source in range(l...]
    dot_general x3 -> x0, matrix products: 58.4 us -> none  [the longest x1 28.6 us: unrotate(): jnp.einsum('rbi,ij->rbj', blocks, hmat, precision=lax.Precision.HIGHEST)]
    mul x18 -> x0, local copies, waits for them, and re-layouts: 46.3 us -> none  [dequant(): return (blocks * scales.astype(jnp.float32)[..., None]).reshape(shape)]
    ppermute x14 -> x0, waiting for transfers between devices: 35.7 us -> none  [passed_along(): lax.ppermute(value, axis, [(source, source + steps) for source in range(l...]
    all_gather x1 -> x0, blocking collectives: 35.1 us -> none  [body(): lax.all_gather(final[1], 'dev', axis=0, tiled=True)]
  transfers between devices with their start and end apart: 18 -> 0, of which waited for: 10 -> 0; matrix products, arithmetic and copies ran while one was open for 11% -> 0% of each run, Pallas kernels for 0% -> 0%
where the time goes in v2:
time: 95.2 us; the launch traced here: 95.1 us
  Pallas kernels  92.4 us (97%)
    pallas_call x1, Pallas kernels, fast(): pl.pallas_call(kernel, out_shape=(jax.ShapeDtypeStruct((OWN, BLOCK), bf16...  87.9 us
    pallas_call x1, Pallas kernels, assemble(): pl.pallas_call(assemble_kernel, out_shape=(jax.ShapeDtypeStruct((OWN, BLO...  4.59 us

profile of v2, /device:TPU:1, one launch (start us, length us, event | category | flops | bytes accessed | tf_op | source)
XLA Modules:
  0.0 95.1 jit_solution(4172848280541450062)
XLA Ops:
  0.6 0.0 copy-start.1
  0.6 87.9 %sync.1 = (bf16[288,128]{1,0:T(8,128)(2,1)}, bf16[3,2,4,4,4,96,128]{6,5,4,3,2,1,0:T(8,128)(2,1)S(1)}, f32[1,1]{1,0:T(1,128)}) custom-call(bf16[320,4608]{1,0:T(8,128)(2,1)} %x_hbm.1, bf16[320,1024]{1,0:T(8,128)(2,1)} %cot_ref.1, s32[1,1024]{1,0:T(1,128)} %bitcast.140), custom_call_target="tpu_custom_call" | custom-call | flops 10000000000 | bytes 30000000 | tf_op jit(solution)/shard_map/sync/pallas_call | solution.py:520
  88.5 0.0 copy-start.5
  88.5 0.0 copy-start
  88.5 0.9 copy-done
  89.4 4.6 %assemble.1 = (bf16[288,128]{1,0:T(8,128)(2,1)}, bf16[4608,1024]{1,0:T(8,128)(2,1)}) custom-call(bf16[3,2,4,4,4,96,128]{6,5,4,3,2,1,0:T(8,128)(2,1)S(1)} %get-tuple-element.83.gat, bf16[288,128]{1,0:T(8,128)(2,1)S(1)} %copy-done), custom_call_target="tpu_custom_call" | custom-call | bytes 20000000 | tf_op jit(solution)/shard_map/assemble/pallas_call | solution.py:606
  94.0 0.0 copy-done.1
  94.0 0.0 copy-done.5
  94.0 0.9 while.13
Async XLA Ops:
  0.6 93.4 %copy-start.1 = (bf16[320,4608]{1,0:T(8,128)(2,1)S(1)}, bf16[320,4608]{1,0:T(8,128)(2,1)}, u32[]{:S(2)}) copy-start(bf16[320,4608]{1,0:T(8,128)(2,1)} %x_hbm.1) | copy-start | bytes 8847364
  88.5 5.5 %copy-start.5 = (s32[1024]{0:T(1024)S(1)}, s32[1024]{0:T(1024)}, u32[]{:S(2)}) copy-start(s32[1024]{0:T(1024)} %param.16) | copy-start | bytes 12292
  88.5 0.9 copy-start

commit v3 on v2

--- a/solution.py
+++ b/solution.py
@@ -19,6 +19,7 @@
 LAG_A, LAG_B, LAG_C, LAG_D = 1, 5, 8, 10
 MAGIC = 12582912.0
 MESH = pl.DeviceIdType.MESH
+GATHERS = (("xyz", 0, 64), ("yzx", 64, 64), ("zxy", 128, 64), ("xyz", 192, 32), ("yzx", 224, 32), ("zxy", 256, 32))
 
 
 def hadamard_in_kernel():
@@ -62,9 +63,9 @@
 
 
 def kernel(
-    x_hbm, cot_ref, sb_ref, rot_ref, gat, bad_ref,
+    x_hbm, cot_hbm, sb_ref, rot_ref, early, late, bad_ref,
     xv, ct3, tmp0, tmp1, tmp2, tmp3, own, out_, got, om, sm, gm, pw, acc, accm,
-    z1, z1m, z1r, z1rm, z2, z2m, z2r, z2rm, xs, xsm, xr, xrm, gbuf, parts, rbuf, rgot, gauge,
+    z1, z1m, z1r, z1rm, z2, z2m, z2r, z2rm, xs, xsm, xr, xrm, gbuf, parts, rbuf, rgot, gauge, cot_ref,
     sib_s, sib_r, z1_s, z1_r, z2_s, z2_r, x_s, x_r, g_s, g_r, r_s, r_r, a_s, a_r, f_r, l_s,
 ):
     g = lax.axis_index("group")
@@ -84,7 +85,9 @@
     column = 2 * k + g // 4
     to_self = jnp.logical_and(k == g // 2, g % 2 == g // 4).astype(jnp.int32)
 
-    fetch = pltpu.make_async_copy(x_hbm, xv, l_s)
+    fetch_cot = pltpu.make_async_copy(cot_hbm, cot_ref, l_s.at[0])
+    fetch_cot.start()
+    fetch = pltpu.make_async_copy(x_hbm, xv, l_s.at[1])
     fetch.start()
 
     bar = pltpu.get_barrier_semaphore()
@@ -108,6 +111,7 @@
 
     hmat = hadamard_in_kernel()
     signs = (2 * sb_ref[...] - 1).astype(jnp.float32)
+    fetch_cot.wait()
     for blk in range(8):
         cols = slice(blk * BLOCK, (blk + 1) * BLOCK)
         signed = (cot_ref[:, cols].astype(jnp.float32) * signs[:, cols]).astype(jnp.bfloat16)
@@ -349,6 +353,68 @@
             for q in range(1, 8):
                 g_copy(div(s, 3), q).start()
 
+    def moved(axis, delta):
+        return (
+            rem(x + delta, 4) if axis == "x" else x,
+            rem(y + delta, 4) if axis == "y" else y,
+            rem(z + delta, 4) if axis == "z" else z,
+        )
+
+    def mine(j, n):
+        return {"x": x, "y": y, "z": z}[GATHERS[j][0][n]]
+
+    def held(j, core, *index):
+        ref, n = (early, j) if j < 3 else (late, j - 3)
+        return ref.at[(n, core) + index]
+
+    def to_mate(j, phase, delta, ref, n):
+        who = dev(*moved(GATHERS[j][0][phase], delta), c)
+        return remote(ref, ref, a_s.at[j, phase], a_r.at[j, n], who)
+
+    def half_slab(j, ring, h):
+        return held(j, c, rem(mine(j, 2) + ring, 4), pl.ds(2 * h, 2))
+
+    def last(j, way, h, ring, n):
+        to_mate(j, 2, way, half_slab(j, ring, h), n).start()
+
+    def forward(j, ring):
+        ref = held(j, c, rem(mine(j, 2) + ring, 4))
+        remote(ref, ref, a_s.at[j, 3], f_r.at[j], sibling).start()
+
+    def phase0(j, mean):
+        block = held(j, c, mine(j, 2), mine(j, 1), mine(j, 0))
+        block[...] = mean
+        for delta in (1, 3, 2):
+            to_mate(j, 0, delta, block, 0).start()
+
+    def phase1(j):
+        took(a_r.at[j, 0], 3 * GATHERS[j][2])
+        for delta in (1, 3, 2):
+            to_mate(j, 1, delta, held(j, c, mine(j, 2), mine(j, 1)), 1).start()
+
+    def phase2(j):
+        took(a_r.at[j, 1], 12 * GATHERS[j][2])
+        last(j, 1, 0, 0, 2)
+        last(j, 3, 1, 0, 3)
+        last(j, 1, 1, 0, 4)
+        last(j, 3, 0, 0, 4)
+        forward(j, 0)
+
+    def relay(j):
+        took(a_r.at[j, 2], 8 * GATHERS[j][2])
+        last(j, 1, 0, 3, 5)
+        took(a_r.at[j, 3], 8 * GATHERS[j][2])
+        last(j, 3, 1, 1, 5)
+
+    def spread(j):
+        took(a_r.at[j, 4], 16 * GATHERS[j][2])
+        forward(j, 3)
+        forward(j, 1)
+
+    def finish(j):
+        took(a_r.at[j, 5], 16 * GATHERS[j][2])
+        forward(j, 2)
+
     fetch.wait()
 
     def loop(t, _):
@@ -394,46 +460,13 @@
     bad = jnp.max(jnp.where(mean == mean, 0.0, 1.0), axis=(0, 1), keepdims=True)
     mean = jnp.where(bad > 0.0, jnp.nan, mean).astype(jnp.bfloat16)
 
-    order = ("xyz", "yzx", "zxy")
-
-    def moved(axis, delta):
-        return (
-            rem(x + delta, 4) if axis == "x" else x,
-            rem(y + delta, 4) if axis == "y" else y,
-            rem(z + delta, 4) if axis == "z" else z,
-        )
-
-    def at(p, core, where):
-        a = {"x": where[0], "y": where[1], "z": where[2]}
-        return (p, core, a[order[p][2]], a[order[p][1]], a[order[p][0]])
-
-    def to_mate(p, phase, delta, ref, n):
-        return remote(ref, ref, a_s.at[p, phase], a_r.at[p, n], dev(*moved(order[p][phase], delta), c))
-
-    def small(p, phase, delta):
-        return to_mate(p, phase, delta, gat.at[at(p, c, (x, y, z))[: 5 - phase]], phase)
-
-    def mine(p, n):
-        return {"x": x, "y": y, "z": z}[order[p][n]]
-
-    def half_slab(p, ring, h):
-        return gat.at[p, c, rem(mine(p, 2) + ring, 4), pl.ds(2 * h, 2)]
-
-    def last(p, way, h, ring, n):
-        return to_mate(p, 2, way, half_slab(p, ring, h), n)
-
-    def forward(p, ring):
-        ref = gat.at[p, c, rem(mine(p, 2) + ring, 4)]
-        return remote(ref, ref, a_s.at[p, 3], f_r.at[p], sibling)
-
-    for p in range(3):
-        gat[at(p, c, (x, y, z))] = mean[p * PART : (p + 1) * PART]
-        for delta in (1, 3, 2):
-            small(p, 0, delta).start()
-    for p in range(3):
-        took(a_r.at[p, 0], 3 * PART)
-        for delta in (1, 3, 2):
-            small(p, 1, delta).start()
+    for j, (_, row, rows) in enumerate(GATHERS):
+        phase0(j, mean[row : row + rows])
+    for j in range(6):
+        phase1(j)
+
+    for j in range(6):
+        phase2(j)
 
     def send_rotated(s, _):
         copy, here, t = r_copy(s)
@@ -451,7 +484,6 @@
         return 0
 
     lax.fori_loop(0, STAGES, send_rotated, 0)
-
     for ref, sem in (
         (out_, sib_s.at[0]), (sm, sib_s.at[1]),
         (z1.at[0:3, :, 0], z1_s.at[0]), (z1m.at[0:3], z1_s.at[1]), (z1.at[0:6], z1_s.at[2]), (z1m.at[0:6], z1_s.at[3]),
@@ -460,23 +492,14 @@
         (gbuf.at[0:7], g_s),
     ):
         pltpu.make_async_copy(ref, ref, sem).wait()
-    for p in range(3):
-        took(a_r.at[p, 1], 12 * PART)
-        last(p, 1, 0, 0, 2).start()
-        last(p, 3, 1, 0, 3).start()
-        last(p, 1, 1, 0, 4).start()
-        last(p, 3, 0, 0, 4).start()
-    for p in range(3):
-        forward(p, 0).start()
-    for p in range(3):
-        took(a_r.at[p, 2], 8 * PART)
-        last(p, 1, 0, 3, 5).start()
-        took(a_r.at[p, 3], 8 * PART)
-        last(p, 3, 1, 1, 5).start()
-    for p in range(3):
-        took(a_r.at[p, 4], 16 * PART)
-        forward(p, 3).start()
-        forward(p, 1).start()
+    for j in range(3):
+        relay(j)
+    for j in range(3):
+        spread(j)
+    for j in range(3, 6):
+        relay(j)
+    for j in range(3, 6):
+        spread(j)
 
     def drain_rotated(u, _):
         t = 9 * k + u
@@ -496,20 +519,19 @@
 
     lax.fori_loop(0, STAGES, drain_rotated, 0)
     rot_ref[...] = rgot[...]
-    for p in range(3):
-        took(a_r.at[p, 5], 16 * PART)
-        forward(p, 2).start()
-    for p in range(3):
-        took(f_r.at[p], 64 * PART)
-    for p in range(3):
-        for n, rows in enumerate((3, 12, 48, 64)):
-            took(a_s.at[p, n], rows * PART)
+    for j in range(6):
+        finish(j)
+    for j in range(6):
+        took(f_r.at[j], 64 * GATHERS[j][2])
+    for j in range(6):
+        for n, blocks in enumerate((3, 12, 48, 64)):
+            took(a_s.at[j, n], blocks * GATHERS[j][2])
     marks = jnp.zeros((16, BLOCK), jnp.float32)
     for core in range(2):
         for i in range(4):
             for j in range(4):
                 for n in range(4):
-                    marks = marks + gat[0, core, i, j, n, 0:16, :].astype(jnp.float32)
+                    marks = marks + late[2, core, i, j, n, 0:16, :].astype(jnp.float32)
     bad_ref[0, 0] = jnp.max(jnp.where(marks == marks, 0.0, 1.0))
 
 
@@ -520,12 +542,14 @@
     return pl.pallas_call(
         kernel,
         out_shape=(
-            jax.ShapeDtypeStruct((OWN, BLOCK), bf16),
-            vmem((3, 2, 4, 4, 4, PART, BLOCK), bf16),
+            vmem((OWN, BLOCK), bf16),
+            vmem((3, 2, 4, 4, 4, 2 * SHARE, BLOCK), bf16),
+            vmem((3, 2, 4, 4, 4, SHARE, BLOCK), bf16),
             jax.ShapeDtypeStruct((1, 1), f32),
         ),
-        in_specs=[pl.BlockSpec(memory_space=pl.ANY)] + [pl.BlockSpec(memory_space=vmem)] * 2,
+        in_specs=[pl.BlockSpec(memory_space=pl.ANY)] * 2 + [pl.BlockSpec(memory_space=vmem)],
         out_specs=(
+            pl.BlockSpec(memory_space=vmem),
             pl.BlockSpec(memory_space=vmem),
             pl.BlockSpec(memory_space=vmem),
             pl.BlockSpec(memory_space=pltpu.SMEM),
@@ -560,24 +584,25 @@
             vmem((OWN, BLOCK), bf16),
             vmem((OWN, BLOCK), bf16),
             vmem((64 * PART, BLOCK), bf16),
+            vmem((TOK, KVW), bf16),
             dma((2,)), dma((STAGES,)),
             dma((4,)), dma((STAGES, 2)),
             dma((4,)), dma((STAGES, 2)),
             dma((4,)), dma((STAGES,)),
             dma, dma((3,)),
             dma((STAGES,)), dma((STAGES,)),
-            dma((3, 4)), dma((3, 6)),
-            dma((3,)), dma,
+            dma((6, 4)), dma((6, 6)),
+            dma((6,)), dma((2,)),
         ],
         compiler_params=pltpu.CompilerParams(
-            collective_id=0, has_side_effects=True, vmem_limit_bytes=47 * 2**20
+            collective_id=0, has_side_effects=True, vmem_limit_bytes=53 * 2**20
         ),
         cost_estimate=pl.CostEstimate(flops=10**10, bytes_accessed=3 * 10**7, transcendentals=0),
         name="sync",
     )(x_act, cotangent, sign_bits.reshape(1, KVW))
 
 
-def assemble_kernel(gat, rot_ref, rot_out, out_hbm, rows, sems):
+def assemble_kernel(early, late, rot_ref, rot_out, out_hbm, rows, sems):
     rot_out[...] = rot_ref[...]
     copies = []
     for quad in range(4):
@@ -587,12 +612,13 @@
                 for g in range(8):
                     xh, z, c = quad // 2, (quad % 2) * 2 + k // 2, k % 2
                     x, y = xh * 2 + g // 4, g % 4
-                    p, r = s // 3, (s % 3) * SHARE
-                    where = ((z, y, x), (x, z, y), (y, x, z))[p]
+                    ref, j, r = (early, s // 2, s % 2 * SHARE) if s < 6 else (late, s - 6, 0)
+                    axes = GATHERS[j if s < 6 else j + 3][0]
+                    where = tuple({"x": x, "y": y, "z": z}[axes[n_axis]] for n_axis in (2, 1, 0))
                     column = 2 * k + g // 4
                     rows[
                         n, y * SHARE : (y + 1) * SHARE, column * BLOCK : (column + 1) * BLOCK
-                    ] = gat[(p, c) + where + (slice(r, r + SHARE),)]
+                    ] = ref[(j, c) + where + (slice(r, r + SHARE),)]
             copies.append(
                 pltpu.make_async_copy(rows.at[n], out_hbm.at[pl.ds(n * BLOCK, BLOCK), :], sems.at[n])
             )
@@ -601,7 +627,7 @@
         copy.wait()
 
 
-def assemble(gathered, rotated):
+def assemble(early, late, rotated):
     vmem = pl.BlockSpec(memory_space=pltpu.VMEM)
     return pl.pallas_call(
         assemble_kernel,
@@ -609,7 +635,7 @@
             jax.ShapeDtypeStruct((OWN, BLOCK), jnp.bfloat16),
             jax.ShapeDtypeStruct((D, KVW), jnp.bfloat16),
         ),
-        in_specs=[vmem, vmem],
+        in_specs=[vmem, vmem, vmem],
         out_specs=(vmem, pl.BlockSpec(memory_space=pl.ANY)),
         scratch_shapes=[
             pltpu.VMEM((4 * STAGES, BLOCK, KVW), jnp.bfloat16),
@@ -618,7 +644,7 @@
         compiler_params=pltpu.CompilerParams(vmem_limit_bytes=24 * 2**20),
         cost_estimate=pl.CostEstimate(flops=0, bytes_accessed=2 * 10**7, transcendentals=0),
         name="assemble",
-    )(gathered, rotated)
+    )(early, late, rotated)
 
 
 def hadamard():
@@ -709,8 +735,8 @@
 
 
 def body(x_act, cotangent, sign_bits):
-    rotated, gathered, inexact = fast(x_act, cotangent, sign_bits)
-    rotated, mean = assemble(gathered, rotated)
+    rotated, early, late, inexact = fast(x_act, cotangent, sign_bits)
+    rotated, mean = assemble(early, late, rotated)
     _, rotated, mean = lax.while_loop(
         lambda state: state[0] > 0.0,
         lambda state: (jnp.float32(0.0), *general(x_act, cotangent, sign_bits)),

time: 95.2 us -> 92.5 us (0.972)
  Pallas kernels: 92.4 us -> 90.6 us
    pallas_call x1, Pallas kernels: 87.9 us -> 86.1 us  [fast(): pl.pallas_call(kernel, out_shape=(vmem((OWN, BLOCK), bf16), vmem((3, 2, 4...]
where the time goes in v3:
time: 92.5 us; the launch traced here: 92.4 us
  Pallas kernels  90.6 us (98%)
    pallas_call x1, Pallas kernels, fast(): pl.pallas_call(kernel, out_shape=(vmem((OWN, BLOCK), bf16), vmem((3, 2, 4...  86.1 us
    pallas_call x1, Pallas kernels, assemble(): pl.pallas_call(assemble_kernel, out_shape=(jax.ShapeDtypeStruct((OWN, BLO...  4.59 us

profile of v3, /device:TPU:1, one launch (start us, length us, event | category | flops | bytes accessed | tf_op | source)
XLA Modules:
  0.0 92.4 jit_solution(3684601054188094593)
XLA Ops:
  0.6 86.1 %sync.1 = (bf16[288,128]{1,0:T(8,128)(2,1)S(1)}, bf16[3,2,4,4,4,64,128]{6,5,4,3,2,1,0:T(8,128)(2,1)S(1)}, bf16[3,2,4,4,4,32,128]{6,5,4,3,2,1,0:T(8,128)(2,1)S(1)}, f32[1,1]{1,0:T(1,128)}) custom-call(bf16[320,4608]{1,0:T(8,128)(2,1)} %x_hbm.1, bf16[320,1024]{1,0:T(8,128)(2,1)} %cot_hbm.1, s32[1,1024]{1,0:T(1,128)} %bitcast.140), custom_call_target="tpu_custom_call" | custom-call | flops 10000000000 | bytes 30000000 | tf_op jit(solution)/shard_map/sync/pallas_call | solution.py:542
  86.7 0.0 copy-start
  86.7 0.0 copy-start.3
  86.7 4.6 %assemble.1 = (bf16[288,128]{1,0:T(8,128)(2,1)}, bf16[4608,1024]{1,0:T(8,128)(2,1)}) custom-call(bf16[3,2,4,4,4,64,128]{6,5,4,3,2,1,0:T(8,128)(2,1)S(1)} %get-tuple-element.84.early, bf16[3,2,4,4,4,32,128]{6,5,4,3,2,1,0:T(8,128)(2,1)S(1)} %get-tuple-element.85.late, bf16[288,128]{1,0:T(8,128)(2,1)S(1)} %get-tuple-element.86.rot_ref), custom_call_target="tpu_custom_call" | custom-call | bytes 20000000 | tf_op jit(solution)/shard_map/assemble/pallas_call | solution.py:632
  91.3 0.0 copy-done
  91.3 0.0 copy-done.3
  91.3 0.9 while.13
Async XLA Ops:
  86.7 4.6 %copy-start = (bf16[320,1024]{1,0:T(8,128)(2,1)S(1)}, bf16[320,1024]{1,0:T(8,128)(2,1)}, u32[]{:S(2)}) copy-start(bf16[320,1024]{1,0:T(8,128)(2,1)} %cot_hbm.1) | copy-start | bytes 1966084
  86.7 4.6 %copy-start.3 = (s32[1024]{0:T(1024)S(1)}, s32[1024]{0:T(1024)}, u32[]{:S(2)}) copy-start(s32[1024]{0:T(1024)} %param.16) | copy-start | bytes 12292

commit v4 on v3

--- a/solution.py
+++ b/solution.py
@@ -16,7 +16,7 @@
 OWN = 288
 PART = 96
 SHARE = 32
-LAG_A, LAG_B, LAG_C, LAG_D = 1, 5, 8, 10
+LAG_A, LAG_B, LAG_C, LAG_D = 1, 4, 8, 11
 MAGIC = 12582912.0
 MESH = pl.DeviceIdType.MESH
 GATHERS = (("xyz", 0, 64), ("yzx", 64, 64), ("zxy", 128, 64), ("xyz", 192, 32), ("yzx", 224, 32), ("zxy", 256, 32))
@@ -445,23 +445,29 @@
 
     lax.fori_loop(0, STAGES + LAG_D, loop, 0)
 
+    my_signs = (2 * sb_ref[:, pl.ds(pl.multiple_of(column * BLOCK, BLOCK), BLOCK)] - 1).astype(jnp.float32)
     parts[g] = gbuf[g]
-    for p in range(3):
-        took(g_r.at[p], 7 * PART)
-    total = parts[0].astype(jnp.float32)
-    for other in range(1, 8):
-        total = total + parts[other].astype(jnp.float32)
-        total = rounded(total, scale_of(jnp.max(jnp.abs(total), axis=1, keepdims=True)))
-    total = total * (1.0 / 128.0)
-    rbuf[...] = total.astype(jnp.bfloat16)
-    turned = jnp.dot(total.astype(jnp.bfloat16), hmat, preferred_element_type=jnp.float32)
-    my_signs = (2 * sb_ref[:, pl.ds(pl.multiple_of(column * BLOCK, BLOCK), BLOCK)] - 1).astype(jnp.float32)
-    mean = turned * (1.0 / BLOCK) * my_signs
-    bad = jnp.max(jnp.where(mean == mean, 0.0, 1.0), axis=(0, 1), keepdims=True)
-    mean = jnp.where(bad > 0.0, jnp.nan, mean).astype(jnp.bfloat16)
-
-    for j, (_, row, rows) in enumerate(GATHERS):
-        phase0(j, mean[row : row + rows])
+
+    def chain(first, end, bad):
+        total = parts[0, first:end, :].astype(jnp.float32)
+        for other in range(1, 8):
+            total = total + parts[other, first:end, :].astype(jnp.float32)
+            total = rounded(total, scale_of(jnp.max(jnp.abs(total), axis=1, keepdims=True)))
+        total = total * (1.0 / 128.0)
+        rbuf[first:end, :] = total.astype(jnp.bfloat16)
+        turned = jnp.dot(total.astype(jnp.bfloat16), hmat, preferred_element_type=jnp.float32)
+        mean = turned * (1.0 / BLOCK) * my_signs
+        bad = jnp.maximum(bad, jnp.max(jnp.where(mean == mean, 0.0, 1.0), axis=(0, 1), keepdims=True))
+        return jnp.where(bad > 0.0, jnp.nan, mean).astype(jnp.bfloat16), bad
+
+    bad = jnp.zeros((1, 1), jnp.float32)
+    for arrived, first, end, gathers in (((0, 1), 0, 2 * PART, (0, 1, 2)), ((2,), 2 * PART, OWN, (3, 4, 5))):
+        for p in arrived:
+            took(g_r.at[p], 7 * PART)
+        mean, bad = chain(first, end, bad)
+        for j in gathers:
+            _, row, rows = GATHERS[j]
+            phase0(j, mean[row - first : row - first + rows])
     for j in range(6):
         phase1(j)
 

time: 92.5 us -> 89.6 us (0.969)
  Pallas kernels: 90.6 us -> 87.7 us
    pallas_call x1, Pallas kernels: 86.1 us -> 83.1 us  [fast(): pl.pallas_call(kernel, out_shape=(vmem((OWN, BLOCK), bf16), vmem((3, 2, 4...]
where the time goes in v4:
time: 89.6 us; the launch traced here: 89.5 us
  Pallas kernels  87.7 us (98%)
    pallas_call x1, Pallas kernels, fast(): pl.pallas_call(kernel, out_shape=(vmem((OWN, BLOCK), bf16), vmem((3, 2, 4...  83.1 us
    pallas_call x1, Pallas kernels, assemble(): pl.pallas_call(assemble_kernel, out_shape=(jax.ShapeDtypeStruct((OWN, BLO...  4.59 us

profile of v4, /device:TPU:1, one launch (start us, length us, event | category | flops | bytes accessed | tf_op | source)
XLA Modules:
  0.0 89.5 jit_solution(17487127272491908119)
XLA Ops:
  0.6 83.1 %sync.1 = (bf16[288,128]{1,0:T(8,128)(2,1)S(1)}, bf16[3,2,4,4,4,64,128]{6,5,4,3,2,1,0:T(8,128)(2,1)S(1)}, bf16[3,2,4,4,4,32,128]{6,5,4,3,2,1,0:T(8,128)(2,1)S(1)}, f32[1,1]{1,0:T(1,128)}) custom-call(bf16[320,4608]{1,0:T(8,128)(2,1)} %x_hbm.1, bf16[320,1024]{1,0:T(8,128)(2,1)} %cot_hbm.1, s32[1,1024]{1,0:T(1,128)} %bitcast.140), custom_call_target="tpu_custom_call" | custom-call | flops 10000000000 | bytes 30000000 | tf_op jit(solution)/shard_map/sync/pallas_call | solution.py:548
  83.8 0.0 copy-start
  83.8 0.0 copy-start.3
  83.8 4.6 %assemble.1 = (bf16[288,128]{1,0:T(8,128)(2,1)}, bf16[4608,1024]{1,0:T(8,128)(2,1)}) custom-call(bf16[3,2,4,4,4,64,128]{6,5,4,3,2,1,0:T(8,128)(2,1)S(1)} %get-tuple-element.84.early, bf16[3,2,4,4,4,32,128]{6,5,4,3,2,1,0:T(8,128)(2,1)S(1)} %get-tuple-element.85.late, bf16[288,128]{1,0:T(8,128)(2,1)S(1)} %get-tuple-element.86.rot_ref), custom_call_target="tpu_custom_call" | custom-call | bytes 20000000 | tf_op jit(solution)/shard_map/assemble/pallas_call | solution.py:638
  88.4 0.0 copy-done
  88.4 0.0 copy-done.3
  88.4 0.9 while.13
Async XLA Ops:
  83.8 4.6 %copy-start = (bf16[320,1024]{1,0:T(8,128)(2,1)S(1)}, bf16[320,1024]{1,0:T(8,128)(2,1)}, u32[]{:S(2)}) copy-start(bf16[320,1024]{1,0:T(8,128)(2,1)} %cot_hbm.1) | copy-start | bytes 1966084
  83.8 4.6 %copy-start.3 = (s32[1024]{0:T(1024)S(1)}, s32[1024]{0:T(1024)}, u32[]{:S(2)}) copy-start(s32[1024]{0:T(1024)} %param.16) | copy-start | bytes 12292
